TPU v7x, 32 devices: a whole 2x2x4 slice. The times are simulated.
32 devices in a mesh: tower: 16 (over z, x, core), batch: 2 (over y).
Axes of the slice: x: 2, y: 2, z: 4, core: 2. Of those that a mesh axis runs over, the one named last changes fastest.
Arguments:
- image_rows: bfloat16 [32, 197, 768], P(('tower', 'batch')), may hold values from -6 to 6
- text_rows: bfloat16 [32, 512, 768], P(('tower', 'batch')), may hold values from -6 to 6
- caption_lengths: int32 [32], replicated, may hold values from 8 to 512, as said below
- concat_cot: bfloat16 [32, 711, 768], P(('tower', 'batch')), may hold values from -6 to 6
- tile_slot: int32 [234], replicated, may hold values from 0 to 255, as said below
- tile_weight: float32 [256, 256, 256], P(('tower', 'batch'))
- tile_first: float32 [256, 256, 256], P(('tower', 'batch'))
- tile_second: float32 [256, 256, 256], P(('tower', 'batch')), as said below
- left_stat: float32 [256, 256, 256], P(('tower', 'batch')), as said below
- right_stat: float32 [256, 256, 256], P(('tower', 'batch')), as said below
- left_basis: float32 [256, 256, 256], P(('tower', 'batch')), as said below
- right_basis: float32 [256, 256, 256], P(('tower', 'batch')), as said below
- vec_weight: float32 [32, 768], P(('tower', 'batch'))
- vec_first: float32 [32, 768], P(('tower', 'batch'))
- vec_second: float32 [32, 768], P(('tower', 'batch')), as said below
Outputs:
- concat: bfloat16 [32, 711, 768], P(('tower', 'batch'))
- image_grad: bfloat16 [32, 197, 768], P(('tower', 'batch'))
- text_grad: bfloat16 [32, 512, 768], P(('tower', 'batch'))
- tile_weight_new: float32 [256, 256, 256], P(('tower', 'batch'))
- tile_first_new: float32 [256, 256, 256], P(('tower', 'batch'))
- tile_second_new: float32 [256, 256, 256], P(('tower', 'batch'))
- left_stat_new: float32 [256, 256, 256], P(('tower', 'batch'))
- right_stat_new: float32 [256, 256, 256], P(('tower', 'batch'))
- left_basis_new: float32 [256, 256, 256], P(('tower', 'batch'))
- right_basis_new: float32 [256, 256, 256], P(('tower', 'batch'))
- vec_weight_new: float32 [32, 768], P(('tower', 'batch'))
- vec_first_new: float32 [32, 768], P(('tower', 'batch'))
- vec_second_new: float32 [32, 768], P(('tower', 'batch'))
Inputs may be any that keep to these rules, and one draw needn't show every extreme that they name: `caption_lengths`: some caption has 512 real rows and some has 8. `tile_slot`: distinct slots; slot 0 and slot 255 are among them; slot s is row s of the tile arrays. `left_basis`: each slot's matrix is orthogonal. `right_basis`: each slot's matrix is orthogonal. `left_stat`: each slot's matrix is symmetric positive definite. `right_stat`: each slot's matrix is symmetric positive definite. `tile_second`: positive entries. `vec_second`: positive entries.
All inputs are finite; a program needn't handle non-finite values.
Results may differ from a plain program's by a relative error of at most 0.014.
The roundings to bfloat16 on the way count: a program that leaves them out, or rounds other values in their place, can miss the bound.
Values may be sent and summed in bfloat16 or wider, within the bound.
A program may use at most 360 MiB of HBM per device.

v0:
```python
import jax
import jax.numpy as jnp
from jax import lax
from jax.sharding import PartitionSpec as P

D = 768
FF = 3072
HEADS = 12
HEAD_DIM = 64
IMG = 197
TXT = 512
MMROWS = 2
TILE_ORDER = 256
STEP = 10


BETA_ONE = 0.9
BETA_TWO = 0.95
EPSILON = 1e-08
RATE_MATRIX = 0.05
RATE_VECTOR = 0.6
DECAY = 0.01
MASKED = -1000000000.0
HIGH = lax.Precision.HIGHEST


def passed_along(value, axis, steps):
    count = lax.axis_size(axis)
    pairs = [(source, (source + steps) % count) for source in range(count)]
    return lax.ppermute(value, axis, pairs)


def rounded(values):
    return values.astype(jnp.bfloat16)


def layer_stats(values):
    center = values - jnp.mean(values, -1, keepdims=True)
    inverse = lax.rsqrt(jnp.mean(center * center, -1, keepdims=True) + 1e-05)
    return (center * inverse, inverse)


def layer_back(grad_normed, normed, inverse):
    return inverse * (
        grad_normed
        - jnp.mean(grad_normed, -1, keepdims=True)
        - normed * jnp.mean(grad_normed * normed, -1, keepdims=True)
    )


def apply_weight(left_rows, matrix):
    return jnp.dot(left_rows, matrix, preferred_element_type=jnp.float32)


def apply_transposed(left_rows, matrix):
    return lax.dot_general(
        left_rows, matrix, (((1,), (1,)), ((), ())), preferred_element_type=jnp.float32
    )


def weight_grad(inputs, grad_rows):
    return lax.dot_general(
        inputs, grad_rows, (((0,), (0,)), ((), ())), preferred_element_type=jnp.float32
    )


def gelu_slope(values):
    cumulative = 0.5 * (1.0 + lax.erf(values * 0.7071067811865476))
    density = jnp.exp(-0.5 * values * values) * 0.3989422804014327
    return cumulative + values * density


def shapes_list():
    return ((D, D), (D, D), (D, D), (D, D), (D, FF), (FF, D), (D, D))


def matrix_of(tile_set, rows_count, cols_count):
    blocks = tile_set.reshape(
        rows_count // TILE_ORDER, cols_count // TILE_ORDER, TILE_ORDER, TILE_ORDER
    )
    return blocks.transpose(0, 2, 1, 3).reshape(rows_count, cols_count)


def tiles_of(matrix):
    rows_count, cols_count = matrix.shape
    blocks = matrix.reshape(
        rows_count // TILE_ORDER, TILE_ORDER, cols_count // TILE_ORDER, TILE_ORDER
    )
    return blocks.transpose(0, 2, 1, 3).reshape(-1, TILE_ORDER, TILE_ORDER)


def matrices_from(tile_set):
    result = []
    offset = 0
    for rows_count, cols_count in shapes_list():
        amount = rows_count // TILE_ORDER * (cols_count // TILE_ORDER)
        result.append(matrix_of(tile_set[offset : offset + amount], rows_count, cols_count))
        offset = offset + amount
    return tuple(result)


def tiles_from(matrices):
    return jnp.concatenate([tiles_of(matrix) for matrix in matrices], 0)


def split_vectors(vectors):
    after = 7 + FF // D
    return (
        vectors[0],
        vectors[1],
        vectors[2],
        vectors[3],
        vectors[4],
        vectors[5],
        vectors[6],
        vectors[7:after].reshape(FF),
        vectors[after],
        vectors[after + 1],
        vectors[after + 2],
        vectors[after + 3],
    )


def tower_pass(matrices, vectors, rows, cotangent, valid):
    w_query, w_key, w_value, w_out, w_up, w_down, w_proj = matrices
    (
        gain_one,
        shift_one,
        bias_query,
        bias_value,
        bias_out,
        gain_two,
        shift_two,
        bias_up,
        bias_down,
        gain_three,
        shift_three,
        bias_proj,
    ) = split_vectors(vectors)
    seq_count, length, row_width = rows.shape
    row_total = seq_count * length
    score_scale = HEAD_DIM ** (-0.5)
    head_shape = (seq_count, length, HEADS, HEAD_DIM)
    flat_rows = rows.reshape(row_total, row_width).astype(jnp.float32)
    keep_rows = valid.reshape(row_total, 1).astype(jnp.float32)
    penalty = jnp.where(valid[:, None, None, :], 0.0, MASKED)
    normed_one, inverse_one = layer_stats(flat_rows)
    input_one = rounded(normed_one * gain_one + shift_one)
    query_heads = rounded(apply_weight(input_one, w_query) + bias_query).reshape(head_shape)
    key_heads = rounded(apply_weight(input_one, w_key)).reshape(head_shape)
    value_heads = rounded(apply_weight(input_one, w_value) + bias_value).reshape(head_shape)

    def scores_of():
        raw_scores = jnp.einsum(
            "sqhe,skhe->shqk", query_heads, key_heads, preferred_element_type=jnp.float32
        )
        return raw_scores * score_scale + penalty

    scores = scores_of()
    highest = jnp.max(scores, -1, keepdims=True)
    log_total = highest + jnp.log(jnp.sum(jnp.exp(scores - highest), -1, keepdims=True))
    weights_soft = rounded(jnp.exp(scores - log_total))
    mixed_rows = rounded(
        jnp.einsum("shqk,skhe->sqhe", weights_soft, value_heads, preferred_element_type=jnp.float32)
    ).reshape(row_total, row_width)
    attended = flat_rows + (apply_weight(mixed_rows, w_out) + bias_out)
    normed_two, inverse_two = layer_stats(attended)
    input_two = rounded(normed_two * gain_two + shift_two)
    upper_pre = apply_weight(input_two, w_up) + bias_up
    hidden = rounded(jax.nn.gelu(upper_pre, approximate=False))
    final_rows = attended + (apply_weight(hidden, w_down) + bias_down)
    normed_three, inverse_three = layer_stats(final_rows)
    input_three = rounded(normed_three * gain_three + shift_three)
    projected = rounded((apply_weight(input_three, w_proj) + bias_proj) * keep_rows)
    grad_output = cotangent.reshape(row_total, row_width).astype(jnp.float32) * keep_rows
    grad_low = rounded(grad_output)
    grad_proj = weight_grad(input_three, grad_low)
    grad_bias_proj = jnp.sum(grad_output, 0)
    grad_three = apply_transposed(grad_low, w_proj)
    grad_gain_three = jnp.sum(grad_three * normed_three, 0)
    grad_shift_three = jnp.sum(grad_three, 0)
    grad_final = layer_back(grad_three * gain_three, normed_three, inverse_three)
    grad_branch = rounded(grad_final)
    grad_down = weight_grad(hidden, grad_branch)
    grad_bias_down = jnp.sum(grad_branch, 0, dtype=jnp.float32)
    grad_hidden = apply_transposed(grad_branch, w_down)
    grad_upper = rounded(grad_hidden * gelu_slope(upper_pre))
    grad_up = weight_grad(input_two, grad_upper)
    grad_bias_up = jnp.sum(grad_upper, 0, dtype=jnp.float32)
    grad_two = apply_transposed(grad_upper, w_up)
    grad_gain_two = jnp.sum(grad_two * normed_two, 0)
    grad_shift_two = jnp.sum(grad_two, 0)
    grad_attended = grad_final + layer_back(grad_two * gain_two, normed_two, inverse_two)
    grad_attn = rounded(grad_attended)
    grad_wout = weight_grad(mixed_rows, grad_attn)
    grad_bias_out = jnp.sum(grad_attn, 0, dtype=jnp.float32)
    grad_mixed = rounded(apply_transposed(grad_attn, w_out)).reshape(head_shape)
    weights_again = jnp.exp(scores_of() - log_total)
    grad_value_heads = rounded(
        jnp.einsum(
            "shqk,sqhe->skhe",
            rounded(weights_again),
            grad_mixed,
            preferred_element_type=jnp.float32,
        )
    )
    grad_weights = jnp.einsum(
        "sqhe,skhe->shqk", grad_mixed, value_heads, preferred_element_type=jnp.float32
    )
    row_dot = jnp.sum(weights_again * grad_weights, -1, keepdims=True)
    grad_scores = rounded(weights_again * (grad_weights - row_dot))
    grad_query_heads = rounded(
        jnp.einsum("shqk,skhe->sqhe", grad_scores, key_heads, preferred_element_type=jnp.float32)
        * score_scale
    )
    grad_key_heads = rounded(
        jnp.einsum("shqk,sqhe->skhe", grad_scores, query_heads, preferred_element_type=jnp.float32)
        * score_scale
    )
    grad_queries = grad_query_heads.reshape(row_total, row_width)
    grad_keys = grad_key_heads.reshape(row_total, row_width)
    grad_values = grad_value_heads.reshape(row_total, row_width)
    grad_wquery = weight_grad(input_one, grad_queries)
    grad_bias_query = jnp.sum(grad_queries, 0, dtype=jnp.float32)
    grad_wkey = weight_grad(input_one, grad_keys)
    grad_wvalue = weight_grad(input_one, grad_values)
    grad_bias_value = jnp.sum(grad_values, 0, dtype=jnp.float32)
    grad_one = (
        apply_transposed(grad_queries, w_query)
        + apply_transposed(grad_keys, w_key)
        + apply_transposed(grad_values, w_value)
    )
    grad_gain_one = jnp.sum(grad_one * normed_one, 0)
    grad_shift_one = jnp.sum(grad_one, 0)
    grad_rows = grad_attended + layer_back(grad_one * gain_one, normed_one, inverse_one)
    first_rows = jnp.stack(
        [
            grad_gain_one,
            grad_shift_one,
            grad_bias_query,
            grad_bias_value,
            grad_bias_out,
            grad_gain_two,
            grad_shift_two,
        ]
    )
    last_rows = jnp.stack([grad_bias_down, grad_gain_three, grad_shift_three, grad_bias_proj])
    vector_grads = jnp.concatenate([first_rows, grad_bias_up.reshape(FF // D, D), last_rows], 0)
    matrix_grads = (grad_wquery, grad_wkey, grad_wvalue, grad_wout, grad_up, grad_down, grad_proj)
    return (
        projected.reshape(seq_count, length, row_width),
        rounded(grad_rows).reshape(seq_count, length, row_width),
        matrix_grads,
        vector_grads,
    )


def orthonormal(matrix):
    gram_matrix = jnp.einsum("nij,nik->njk", matrix, matrix, precision=HIGH)
    lower_factor = jnp.linalg.cholesky(gram_matrix)
    solved = jax.scipy.linalg.solve_triangular(lower_factor, jnp.swapaxes(matrix, 1, 2), lower=True)
    return jnp.swapaxes(solved, 1, 2)


def tile_update(
    grad_tiles, weight, first_moment, second_moment, left_side, right_side, left_rot, right_rot
):
    left_new = BETA_TWO * left_side + (1.0 - BETA_TWO) * jnp.einsum(
        "nij,nkj->nik", grad_tiles, grad_tiles, precision=HIGH
    )
    right_new = BETA_TWO * right_side + (1.0 - BETA_TWO) * jnp.einsum(
        "nji,njk->nik", grad_tiles, grad_tiles, precision=HIGH
    )
    half_turn = jnp.einsum("nji,njk->nik", left_rot, grad_tiles, precision=HIGH)
    turned = jnp.einsum("nij,njk->nik", half_turn, right_rot, precision=HIGH)
    first_new = BETA_ONE * first_moment + (1.0 - BETA_ONE) * turned
    second_new = BETA_TWO * second_moment + (1.0 - BETA_TWO) * turned * turned
    scaled = (
        first_new
        / (1.0 - BETA_ONE**STEP)
        / (jnp.sqrt(second_new / (1.0 - BETA_TWO**STEP)) + EPSILON)
    )
    back_half = jnp.einsum("nij,njk->nik", left_rot, scaled, precision=HIGH)
    direction = jnp.einsum("nij,nkj->nik", back_half, right_rot, precision=HIGH)
    weight_new = weight - RATE_MATRIX * (direction + DECAY * weight)
    left_rot_new = orthonormal(jnp.einsum("nij,njk->nik", left_new, left_rot, precision=HIGH))
    right_rot_new = orthonormal(jnp.einsum("nij,njk->nik", right_new, right_rot, precision=HIGH))
    return (weight_new, first_new, second_new, left_new, right_new, left_rot_new, right_rot_new)


def vector_update(grad_rows, weight, first_moment, second_moment):
    first_new = BETA_ONE * first_moment + (1.0 - BETA_ONE) * grad_rows
    second_new = BETA_TWO * second_moment + (1.0 - BETA_TWO) * grad_rows * grad_rows
    step_size = (
        first_new
        / (1.0 - BETA_ONE**STEP)
        / (jnp.sqrt(second_new / (1.0 - BETA_TWO**STEP)) + EPSILON)
    )
    return (weight - RATE_VECTOR * step_size, first_new, second_new)


def per_device(
    image_rows,
    text_rows,
    caption_lengths,
    concat_cot,
    tile_slot,
    tile_weight,
    tile_first,
    tile_second,
    left_stat,
    right_stat,
    left_basis,
    right_basis,
    vec_weight,
    vec_first,
    vec_second,
):
    tower_count = lax.axis_size("tower")
    batch_count = lax.axis_size("batch")
    device_count = tower_count * batch_count
    half_size = tower_count // 2
    tower_pos = lax.axis_index("tower")
    batch_pos = lax.axis_index("batch")
    is_image = tower_pos < half_size
    tower_side = (tower_pos >= half_size).astype(jnp.int32)
    pairs_here = image_rows.shape[0]
    tiles_tower = tile_slot.shape[0] // 2
    vec_tower = 11 + FF // D
    own_block = tower_pos * batch_count + batch_pos
    partner_block = (tower_pos + half_size) % tower_count * batch_count + batch_pos
    own_lengths = lax.dynamic_slice_in_dim(caption_lengths, own_block * pairs_here, pairs_here)
    partner_lengths = lax.dynamic_slice_in_dim(
        caption_lengths, partner_block * pairs_here, pairs_here
    )
    my_slots = lax.dynamic_slice_in_dim(tile_slot, tower_side * tiles_tower, tiles_tower)
    pad_width = ((0, 0), (0, TXT - IMG), (0, 0))
    cot_image = concat_cot[:, MMROWS : MMROWS + IMG]
    cot_text = concat_cot[:, MMROWS + IMG :]
    send_rows = jnp.where(is_image, text_rows, jnp.pad(image_rows, pad_width))
    send_cot = jnp.where(is_image, cot_text, jnp.pad(cot_image, pad_width))
    got_rows, got_cot = passed_along((send_rows, send_cot), "tower", half_size)
    micro_inputs = (
        (image_rows, text_rows, cot_image, cot_text, own_lengths),
        (got_rows[:, :IMG], got_rows, got_cot[:, :IMG], got_cot, partner_lengths),
    )
    learned_total = jnp.sum(concat_cot[:, :MMROWS], 0, dtype=jnp.float32)
    learned_parts = (learned_total, jnp.zeros_like(learned_total))
    kept_weights = None
    micro_results = []
    reduced = None
    weights_set = kept_weights
    for micro_step in range(2):
        tile_low, vec_low = (
            lax.all_gather(
                tile_weight.astype(jnp.bfloat16), ("tower", "batch"), axis=0, tiled=True
            ),
            lax.all_gather(vec_weight.astype(jnp.bfloat16), ("tower", "batch"), axis=0, tiled=True),
        )
        selected_slots = jnp.take(tile_low, my_slots, axis=0)
        unpack_vectors = lax.dynamic_slice_in_dim(
            vec_low, tower_side * vec_tower, vec_tower
        ).astype(jnp.float32)
        unpack_learned = vec_low[2 * vec_tower : 2 * vec_tower + MMROWS]
        weights_set = (matrices_from(selected_slots), unpack_vectors, unpack_learned)
        matrices, vectors, learned = weights_set

        def image_side(inputs):
            img_part, txt_part, img_cot, txt_cot, lengths_here = inputs
            valid = jnp.ones(img_part.shape[:2], jnp.bool_)
            projected, grad_input, matrix_grads, vector_grads = tower_pass(
                matrices, vectors, img_part, img_cot, valid
            )
            return (
                projected,
                jnp.zeros_like(txt_part),
                grad_input,
                jnp.zeros_like(txt_part),
                matrix_grads,
                vector_grads,
            )

        def text_side(inputs):
            img_part, txt_part, img_cot, txt_cot, lengths_here = inputs
            valid = lax.broadcasted_iota(jnp.int32, txt_part.shape[:2], 1) < lengths_here[:, None]
            projected, grad_input, matrix_grads, vector_grads = tower_pass(
                matrices, vectors, txt_part, txt_cot, valid
            )
            return (
                jnp.zeros_like(img_part),
                projected,
                jnp.zeros_like(img_part),
                grad_input,
                matrix_grads,
                vector_grads,
            )

        outcome = lax.cond(is_image, image_side, text_side, micro_inputs[micro_step])
        micro_results.append(outcome[:4])
        tile_terms = jnp.zeros(
            (device_count * tile_weight.shape[0], TILE_ORDER, TILE_ORDER), jnp.float32
        )
        tile_terms = tile_terms.at[my_slots].set(tiles_from(outcome[4]))
        vec_terms = jnp.zeros((device_count * vec_weight.shape[0], D), jnp.float32)
        vec_terms = lax.dynamic_update_slice_in_dim(
            vec_terms, outcome[5], tower_side * vec_tower, 0
        )
        vec_terms = vec_terms.at[2 * vec_tower : 2 * vec_tower + MMROWS].set(
            learned_parts[micro_step]
        )
        tile_terms, vec_terms = (tile_terms, vec_terms)
        tile_part, vec_part = (
            lax.psum_scatter(tile_terms, ("tower", "batch"), scatter_dimension=0, tiled=True),
            lax.psum_scatter(vec_terms, ("tower", "batch"), scatter_dimension=0, tiled=True),
        )
        if micro_step == 0:
            reduced = (tile_part, vec_part)
        else:
            reduced = (reduced[0] + tile_part, reduced[1] + vec_part)
    first_out, second_out = micro_results
    send_proj = jnp.where(is_image, jnp.pad(second_out[0], pad_width), second_out[1])
    send_grad = jnp.where(is_image, jnp.pad(second_out[2], pad_width), second_out[3])
    back_proj, back_grad = passed_along((send_proj, send_grad), "tower", half_size)
    proj_image = jnp.where(is_image, first_out[0], back_proj[:, :IMG])
    proj_text = jnp.where(is_image, back_proj, first_out[1])
    image_grad = jnp.where(is_image, first_out[2], back_grad[:, :IMG])
    text_grad = jnp.where(is_image, back_grad, first_out[3])
    learned_rows = weights_set[2][None]
    concat = jnp.concatenate([learned_rows, proj_image, proj_text], 1)
    tile_grad, vec_grad = reduced
    tile_states = tile_update(
        tile_grad,
        tile_weight,
        tile_first,
        tile_second,
        left_stat,
        right_stat,
        left_basis,
        right_basis,
    )
    vec_states = vector_update(vec_grad, vec_weight, vec_first, vec_second)
    return (
        concat,
        image_grad,
        text_grad,
        tile_states[0],
        tile_states[1],
        tile_states[2],
        tile_states[3],
        tile_states[4],
        tile_states[5],
        tile_states[6],
        vec_states[0],
        vec_states[1],
        vec_states[2],
    )


def solution(mesh):
    return jax.shard_map(
        per_device,
        mesh=mesh,
        in_specs=(
            P(("tower", "batch"), None, None),
            P(("tower", "batch"), None, None),
            P(),
            P(("tower", "batch"), None, None),
            P(),
            P(("tower", "batch"), None, None),
            P(("tower", "batch"), None, None),
            P(("tower", "batch"), None, None),
            P(("tower", "batch"), None, None),
            P(("tower", "batch"), None, None),
            P(("tower", "batch"), None, None),
            P(("tower", "batch"), None, None),
            P(("tower", "batch"), None),
            P(("tower", "batch"), None),
            P(("tower", "batch"), None),
        ),
        out_specs=(
            P(("tower", "batch"), None, None),
            P(("tower", "batch"), None, None),
            P(("tower", "batch"), None, None),
            P(("tower", "batch"), None, None),
            P(("tower", "batch"), None, None),
            P(("tower", "batch"), None, None),
            P(("tower", "batch"), None, None),
            P(("tower", "batch"), None, None),
            P(("tower", "batch"), None, None),
            P(("tower", "batch"), None, None),
            P(("tower", "batch"), None),
            P(("tower", "batch"), None),
            P(("tower", "batch"), None),
        ),
        check_vma=False,
    )
```

profile of v0, /device:TPU:18, one launch (start us, length us, event | category | flops | bytes accessed | tf_op | source)
XLA Modules:
  0.0 3520.1 jit_solution(3195528262043060434)
XLA Ops:
  17.5 171.2 %all-gather = bf16[32,1,768]{2,1,0:T(2,128)(2,1)S(1)} all-gather(bf16[1,1,768]{2,1,0:T(2,128)(2,1)S(1)} %convert_bitcast_fusion.4), channel_id=1, replica_groups=mesh['tower'=16,'batch'=2] {'tower','batch'}, dimensions={0}, use_global_device_ids=true | all-gather | bytes 50688 | tf_op jit(solution)/shard_map/all_gather | solution.py:358
  190.0 65.9 %all-gather.3.cloned.1.call-done = bf16[256,256,256]{2,1,0:T(8,128)(2,1)} async-done(((bf16[8,256,256]{2,1,0:T(8,128)(2,1)}), bf16[256,256,256]{2,1,0:T(8,128)(2,1)}) %all-gather.3.cloned.1.call-update) | async-done | bytes 33554448 | tf_op jit(solution)/shard_map/all_gather | solution.py:355
  323.1 169.0 %conditional.2 = (bf16[1,197,768]{2,1,0:T(8,128)(2,1)}, bf16[1,512,768]{2,1,0:T(8,128)(2,1)}, bf16[1,197,768]{2,1,0:T(8,128)(2,1)}, bf16[1,512,768]{2,1,0:T(8,12...) conditional(s32[]{:T(128)} %convert_element_type.534, ...), branch_computations={%region_0.29_spmd, %region_28.57_spmd} | conditional | flops 26230630400 | bytes 588202112 | solution.py:398
  370.4 18.9 fusion.4
  537.2 13.7 copy.491
  594.6 177.1 %conditional.3 = (bf16[1,512,768]{2,1,0:T(8,128)(2,1)}, bf16[1,512,768]{2,1,0:T(8,128)(2,1)S(1)}, f32[768,768]{1,0:T(8,128)}, f32[768,768]{1,0:T(8,128)}, f32[76...) conditional(s32[]{:T(128)} %convert_element_type.534, ...), branch_computations={%region_56.85_spmd.clone.clone, %region_84.113_spmd} | conditional | flops 26230630400 | bytes 567153536 | solution.py:398
  644.3 18.9 fusion.213
  817.3 13.7 copy.499
  921.1 21.2 broadcast.1236.clone
  942.3 55.7 %scatter_fusion = f32[256,256,256]{2,1,0:T(8,128)} fusion(f32[256,256,256]{2,1,0:T(8,128)} %broadcast.1236.clone, s32[117]{0:T(128)S(1)} %copy-done.146, f32[117,256,256]{2,1,0:T(8,128)} %constant_dynamic-update-slice_fusion), kind=kCustom, calls=%fused_computation.1 | custom fusion | bytes 92013008 | tf_op jit(solution)/shard_map/scatter | solution.py:403
  998.0 21.1 broadcast.1236.clone.1
  1019.1 55.5 %scatter_fusion.1 = f32[256,256,256]{2,1,0:T(8,128)} fusion(f32[256,256,256]{2,1,0:T(8,128)} %broadcast.1236.clone.1, s32[117]{0:T(128)S(1)} %copy-done.146, f32[117,256,256]{2,1,0:T(8,128)} %constant_dynamic-update-slice_fusion.7), kind=kCustom, calls=%fused_computation.2 | custom fusion | bytes 92013008 | tf_op jit(solution)/shard_map/scatter | solution.py:403
  1074.6 64.7 %add.843 = f32[256,256,256]{2,1,0:T(8,128)} add(f32[256,256,256]{2,1,0:T(8,128)} %scatter_fusion, f32[256,256,256]{2,1,0:T(8,128)} %scatter_fusion.1) | non-fusion elementwise | flops 16777216 | bytes 201326592 | tf_op jit(solution)/shard_map/add | solution.py:419
  1148.1 45.4 %collective-permute-done.2 = bf16[1,512,768]{2,1,0:T(8,128)(2,1)} collective-permute-done((bf16[1,512,768]{2,1,0:T(8,128)(2,1)}, bf16[1,512,768]{2,1,0:T(8,128)(2,1)}, u32[]{:S(2)}, u32[]{:S(2)}) %collective-permute-start.2) | collective-permute-done | bytes 786464 | tf_op jit(solution)/shard_map/ppermute | solution.py:30
  1197.0 13.0 collective-permute-done.3
  1211.7 1330.2 %reduce-scatter.2.cloned.1.call-done = f32[8,256,256]{2,1,0:T(8,128)} async-done(((f32[256,256,256]{2,1,0:T(8,128)}), f32[8,256,256]{2,1,0:T(8,128)}) %reduce-scatter.2.cloned.1.call-update) | async-done | bytes 2097168 | tf_op jit(solution)/shard_map/reduce_scatter | solution.py:413
  2582.7 93.8 %custom-call.21 = f32[8,128,128]{2,1,0:T(8,128)S(1)} custom-call(f32[8,128,128]{2,1,0:T(8,128)S(1)} %cholesky.201), custom_call_target="Cholesky" | custom-call | tf_op jit(solution)/shard_map/jit(cholesky)/cholesky | solution.py:260
  2691.1 94.9 %custom-call.17 = f32[8,128,128]{2,1,0:T(8,128)S(1)} custom-call(f32[8,128,128]{2,1,0:T(8,128)} %cholesky.198), custom_call_target="Cholesky" | custom-call | tf_op jit(solution)/shard_map/jit(cholesky)/cholesky | solution.py:260
  2788.6 80.0 %custom-call.22 = f32[8,1,128,128]{2,3,1,0:T(8,128)} custom-call(f32[8,1,128,128]{3,2,1,0:T(8,128)} %get-tuple-element.924), custom_call_target="InvertDiagBlocksLowerTriangular" | custom-call | tf_op jit(solution)/shard_map/jit(cholesky)/cholesky | solution.py:260
  2874.3 95.2 %custom-call.23 = f32[8,128,128]{2,1,0:T(8,128)} custom-call(f32[8,128,128]{2,1,0:T(8,128)} %convolution_subtract_fusion.2), custom_call_target="Cholesky" | custom-call | tf_op jit(solution)/shard_map/jit(cholesky)/cholesky | solution.py:260
  2971.1 80.2 %custom-call.18 = f32[8,1,128,128]{2,3,1,0:T(8,128)} custom-call(f32[8,1,128,128]{3,2,1,0:T(8,128)} %get-tuple-element.925), custom_call_target="InvertDiagBlocksLowerTriangular" | custom-call | tf_op jit(solution)/shard_map/jit(cholesky)/cholesky | solution.py:260
  3057.1 95.2 %custom-call.19 = f32[8,128,128]{2,1,0:T(8,128)} custom-call(f32[8,128,128]{2,1,0:T(8,128)} %convolution_subtract_fusion.3), custom_call_target="Cholesky" | custom-call | tf_op jit(solution)/shard_map/jit(cholesky)/cholesky | solution.py:260
  3167.5 158.2 %custom-call.20 = f32[8,2,128,128]{2,3,1,0:T(8,128)S(1)} custom-call(f32[8,2,128,128]{3,2,1,0:T(8,128)} %bitcast.838), custom_call_target="InvertDiagBlocksLowerTriangular" | custom-call | tf_op jit(solution)/shard_map/jit(_solve_triangular)/vmap()/triangular_solve | solution.py:261
  3344.3 158.0 %custom-call.24 = f32[8,2,128,128]{2,3,1,0:T(8,128)S(1)} custom-call(f32[8,2,128,128]{3,2,1,0:T(8,128)} %bitcast.837), custom_call_target="InvertDiagBlocksLowerTriangular" | custom-call | tf_op jit(solution)/shard_map/jit(_solve_triangular)/vmap()/triangular_solve | solution.py:261
  (564 shorter events, 717.6 us)
Async XLA Ops:
  7.2 2540.6 %copy-start = (f32[8,256,256]{2,1,0:T(8,128)S(1)}, f32[8,256,256]{2,1,0:T(8,128)}, u32[]{:S(2)}) copy-start(f32[8,256,256]{2,1,0:T(8,128)} %param.39) | copy-start | bytes 6291460
  7.2 248.6 %all-gather.3.cloned.1.call-start = ((), (), s32[]{:S(2)}) async-start(), calls=%async_computation.1 | async-start | bytes 34603008 | tf_op jit(solution)/shard_map/all_gather | solution.py:355
  10.1 1136.6 %all-reduce.9.cloned.1.call-start = ((), (), s32[]{:S(2)}) async-start(), calls=%async_computation.3 | async-start | bytes 196608
  10.2 179.2 %copy-start.149 = (s32[234]{0:T(256)S(1)}, s32[234]{0:T(256)}, u32[]{:S(2)}) copy-start(s32[234]{0:T(256)} %param.32) | copy-start | bytes 2812
  11.3 583.3 %collective-permute-start = (bf16[1,512,768]{2,1,0:T(8,128)(2,1)}, bf16[1,512,768]{2,1,0:T(8,128)(2,1)}, u32[]{:S(2)}, u32[]{:S(2)}) collective-permute-start(bf16[1,512,768]{2,1,0:T(8,128)(2,1)} %pad_select_fusion.1), channel_id=1, source_target_pairs={{0,16},{2,18},{4,20},{6,22},{8,24},{10,26},{12,28},{14,30},{16,0},... | collective-permute-start | bytes 2359304 | tf_op jit(solution)/shard_map/ppermute | solution.py:30
  14.9 579.7 %collective-permute-start.1 = (bf16[1,512,768]{2,1,0:T(8,128)(2,1)}, bf16[1,512,768]{2,1,0:T(8,128)(2,1)}, u32[]{:S(2)}, u32[]{:S(2)}) collective-permute-start(bf16[1,512,768]{2,1,0:T(8,128)(2,1)} %get-tuple-element.919), channel_id=1, source_target_pairs={{0,16},{2,18},{4,20},{6,22},{8,24},{10,26},{12,28},{14,30},{16,0},... | collective-permute-start | bytes 2359304 | tf_op jit(solution)/shard_map/ppermute | solution.py:30
  352.9 9.8 copy-start.29
  370.4 18.9 copy-start.78
  420.0 11.4 slice-start
  420.0 11.4 slice-start.1
  420.0 12.6 slice-start.2
  625.5 9.8 copy-start.31
  644.3 18.9 copy-start.80
  693.2 11.4 slice-start.3
  693.2 11.3 slice-start.4
  693.2 12.6 slice-start.5
  875.1 1666.8 %reduce-scatter.2.cloned.1.call-start = ((), (), s32[]{:S(2)}) async-start(), calls=%async_computation.2 | async-start | bytes 69206016 | tf_op jit(solution)/shard_map/reduce_scatter | solution.py:413
  881.5 10.5 slice-start.6
  892.0 14.4 slice-start.9
  892.0 14.4 slice-start.10
  921.1 21.2 copy-start.146
  1141.6 51.9 %collective-permute-start.2 = (bf16[1,512,768]{2,1,0:T(8,128)(2,1)}, bf16[1,512,768]{2,1,0:T(8,128)(2,1)}, u32[]{:S(2)}, u32[]{:S(2)}) collective-permute-start(bf16[1,512,768]{2,1,0:T(8,128)(2,1)} %broadcast_select_fusion.4), channel_id=1, source_target_pairs={{0,16},{2,18},{4,20},{6,22},{8,24},{10,26},{12,28},{14,30},{16,0},... | collective-permute-start | bytes 2359304 | tf_op jit(solution)/shard_map/ppermute | solution.py:30
  1142.7 67.3 %collective-permute-start.3 = (bf16[1,512,768]{2,1,0:T(8,128)(2,1)}, bf16[1,512,768]{2,1,0:T(8,128)(2,1)S(1)}, u32[]{:S(2)}, u32[]{:S(2)}) collective-permute-start(bf16[1,512,768]{2,1,0:T(8,128)(2,1)} %broadcast_select_fusion.2), channel_id=1, source_target_pairs={{0,16},{2,18},{4,20},{6,22},{8,24},{10,26},{12,28},{14,30},{16,0},... | collective-permute-start | bytes 2359304 | tf_op jit(solution)/shard_map/ppermute | solution.py:30
  1194.5 16.3 copy-start.117
  (107 other events, 420.5 us)
Sparse Core Ops, SparseCore 0:
  11.7 244.0 all-gather.2
  875.3 121.2 all-reduce.8
  1139.5 1402.3 reduce-scatter.1
where the time goes:
time: 3530 us; the launch traced here: 3520 us
  waiting for transfers between devices  1450 us (41%)
  other arithmetic  1020 us (29%)
  local copies, waits for them, and re-layouts  536 us (15%)
  matrix products  280 us (8%)
  blocking collectives  171 us (5%)
  loops' own time  36.1 us (1%)
    reduce_scatter x1, waiting for transfers between devices, per_device(): lax.psum_scatter(tile_terms, ('tower', 'batch'), scatter_dimension=0, til...  1330 us
    another operation x14, other arithmetic, orthonormal(): lower_factor = jnp.linalg.cholesky(gram_matrix)  543 us
    another operation x5, other arithmetic, orthonormal(): jax.scipy.linalg.solve_triangular(lower_factor, jnp.swapaxes(matrix, 1, 2...  321 us
    all_gather x1, blocking collectives, per_device(): lax.all_gather(vec_weight.astype(jnp.bfloat16), ('tower', 'batch'), axis=...  171 us
    scatter x2, local copies, waits for them, and re-layouts, per_device(): tile_terms = tile_terms.at[my_slots].set(tiles_from(outcome[4]))  111 us
    reshape x14, local copies, waits for them, and re-layouts, tiles_of(): matrix.reshape(rows_count // TILE_ORDER, TILE_ORDER, cols_count // TILE_O...  93.8 us
    transpose x14, local copies, waits for them, and re-layouts, tiles_of(): return blocks.transpose(0, 2, 1, 3).reshape(-1, TILE_ORDER, TILE_ORDER)  87.3 us
    unnamed x131, local copies, waits for them, and re-layouts  81 us
  transfers between devices with their start and end apart: 7, of which 4 were waited for; matrix products, arithmetic and copies ran while one was open for 17% of the time, Pallas kernels for 0%

commit v1 on v0

v1 whole, which is shorter than its diff:
```python
import functools
import heapq
import itertools

import jax
import jax.numpy as jnp
from jax import lax
from jax.experimental import pallas as pl
from jax.experimental.pallas import tpu as pltpu
from jax.sharding import PartitionSpec as P

BETA_ONE = 0.9
BETA_TWO = 0.95
EPSILON = 1e-08
RATE_MATRIX = 0.05
RATE_VECTOR = 0.6
DECAY = 0.01
STEP = 10
D = 768
FF = 3072
HEADS = 12
HEAD_DIM = 64
IMG = 197
TXT = 512
MMROWS = 2
T = 256
EXTRA = 16
VECS = 11 + FF // D
MASKED = -1000000000.0
NN = (((1,), (0,)), ((), ()))
NT = (((1,), (1,)), ((), ()))
TN = (((0,), (0,)), ((), ()))
KB = D // T
FB = FF // T
WIDE = 2 * T
SET = 2 * KB * WIDE // T


def mm(a, b, dims=NN):
    return lax.dot_general(a, b, dims, preferred_element_type=jnp.float32)


def rounded(v):
    return v.astype(jnp.bfloat16)


def stats(v):
    center = v - jnp.mean(v, -1, keepdims=True)
    inverse = lax.rsqrt(jnp.mean(center * center, -1, keepdims=True) + 1e-05)
    return center * inverse, inverse


def norm_back(grad, normed, inverse):
    return inverse * (
        grad
        - jnp.mean(grad, -1, keepdims=True)
        - normed * jnp.mean(grad * normed, -1, keepdims=True)
    )


def thirds(v):
    high = rounded(v)
    v = v - high.astype(jnp.float32)
    middle = rounded(v)
    return high, middle, rounded(v - middle.astype(jnp.float32))


def tower_body(is_text, rows, slots, slot_ref, length_ref, x_ref, cot_ref, copies, *rest):
    if is_text:
        zi_ref, _, cat_ref, dx_ref, grads = rest[:5]
        z_ref = None
    else:
        z_ref, dx_ref, grads = rest[:3]
        blank, blank_sem = rest[-2:]
        rest = rest[:-2]
    (wqkv, wo, wu, wd, wp, n1, n1t, qkv, qt, o, ot, a, n2, n2t, slope, h, ht, y, n3, n3t,
     cat, da, dqkv, logs, stage, vec_low, vec_all, bias_up, vec_out,
     wsem, stage_sem, vec_sem, vec_out_sem) = rest[5 if is_text else 3 :]
    dy = cat.at[pl.ds(0, rows)]
    dyb, dab, do, dot_, du = n3, n2, o, n3t, h
    first_tile = slot_ref.shape[0] // 2 if is_text else 0
    first_vec = VECS if is_text else 0
    real = TXT if is_text else IMG
    chunk = 64 if is_text else 16
    chunks = [(i * chunk, min((i + 1) * chunk, real)) for i in range(rows // chunk)]
    if is_text:
        length = length_ref[lax.axis_index("tower") * lax.axis_size("batch") + lax.axis_index("batch")]
    else:
        length = IMG
    tile_rows = slots * T

    def padded(value):
        short = chunk - value.shape[0]
        if short:
            value = jnp.concatenate([value, jnp.zeros((short, D), value.dtype)], 0)
        return value

    def x_of(c):
        return padded(x_ref[0, c[0] : c[1], :].astype(jnp.float32))

    def g_of(c):
        begin = c[0] + MMROWS + (IMG if is_text else 0)
        base = begin // 16 * 16
        end = min(-(-(begin + chunk) // 16) * 16, begin + c[1] - c[0])
        value = cot_ref[0, base:end, :].astype(jnp.float32)
        return padded(value[begin - base : begin - base + c[1] - c[0]])

    def at_slot(ref, slot):
        return ref.at[slot // slots, pl.ds(pl.multiple_of(slot % slots * T, T), T), :]

    extra = pl.ds(tile_rows, EXTRA)
    vec_count = VECS + MMROWS if is_text else VECS
    for i in range(vec_count):
        pltpu.make_async_copy(copies.at[first_vec + i, extra], vec_low.at[i], vec_sem).start()
    mats = [(wqkv, 0), (wqkv, D), (wqkv, 2 * D), (wo, 0), (wu, 0), (wd, 0), (wp, 0)]
    shapes = [(KB, KB)] * 4 + [(KB, FB), (FB, KB), (KB, KB)]
    starts = [0]
    for rb, cb in shapes:
        starts.append(starts[-1] + rb * cb)

    def load(which, sem):
        ref, shift = mats[which]
        rb, cb = shapes[which]

        def one(i, _):
            slot = slot_ref[first_tile + starts[which] + i]
            r, c = i // cb, i % cb
            pltpu.make_async_copy(
                at_slot(copies, slot),
                ref.at[pl.ds(pl.multiple_of(r * T, T), T), pl.ds(pl.multiple_of(shift + c * T, T), T)],
                wsem.at[sem],
            ).start()
            return 0

        lax.fori_loop(0, rb * cb, one, 0)

    def drain(ref, sem):
        pltpu.make_async_copy(ref, ref, sem).wait()

    for which, sem in enumerate((0, 0, 0, 1, 2, 3, 4)):
        load(which, sem)
    if not is_text:
        blank[...] = jnp.zeros(blank.shape, blank.dtype)

        def clear(i, _):
            pltpu.make_async_copy(blank, grads.at[i], blank_sem).start()
            return 0

        lax.fori_loop(0, grads.shape[0], clear, 0)

    def put(place, tiles):
        for n, (_, value) in enumerate(tiles):
            stage[place, n] = rounded(value)
        for n, (tile, _) in enumerate(tiles):
            slot = slot_ref[first_tile + tile]
            pltpu.make_async_copy(stage.at[place, n], at_slot(grads, slot), stage_sem.at[place]).start()

    def free(place, count):
        drain(stage.at[place, pl.ds(0, count)], stage_sem.at[place])

    def square(which, product):
        return [
            (starts[which] + r * KB + k, product[r * T : (r + 1) * T, k * T : (k + 1) * T])
            for r in range(KB)
            for k in range(KB)
        ]

    drain(vec_low.at[pl.ds(0, vec_count)], vec_sem)
    for i in range(vec_count):
        line = jnp.concatenate([vec_low[i, k : k + 1, :] for k in range(KB)], 1).astype(jnp.float32)
        vec_all[i : i + 1, :] = line
        if 7 <= i < 7 + FF // D:
            bias_up[:, (i - 7) * D : (i - 6) * D] = line

    def vec(i):
        return vec_all[i : i + 1, :]

    def vec_grad(i, line):
        line = rounded(line)
        parts = [line[:, k * T : (k + 1) * T] for k in range(KB)]
        parts.append(jnp.zeros((EXTRA - KB, T), jnp.bfloat16))
        vec_out[i] = jnp.concatenate(parts, 0)
        pltpu.make_async_copy(vec_out.at[i], grads.at[first_vec + i, extra], vec_out_sem).start()

    for c in chunks:
        normed, _ = stats(x_of(c))
        n1[c[0] : c[0] + chunk, :] = rounded(normed * vec(0) + vec(1))
    n1t[...] = n1[...].T
    drain(wqkv, wsem.at[0])
    scale = HEAD_DIM ** (-0.5)
    qkv[:, :D] = rounded((mm(n1[...], wqkv[:, :D]) + vec(2))) * jnp.asarray(scale, jnp.bfloat16)
    qkv[:, D : 2 * D] = rounded(mm(n1[...], wqkv[:, D : 2 * D]))
    qkv[:, 2 * D :] = rounded(mm(n1[...], wqkv[:, 2 * D :]) + vec(3))
    qt[...] = qkv[:, :D].T
    lane = lax.broadcasted_iota(jnp.int32, (rows, 2 * HEAD_DIM), 1)
    keys = lax.broadcasted_iota(jnp.int32, (rows, 2 * HEAD_DIM), 0)
    penalty = jnp.where(keys < length, 0.0, MASKED).astype(jnp.bfloat16)
    one = jnp.ones((rows, 2 * HEAD_DIM), jnp.bfloat16)
    zero = jnp.zeros((rows, 2 * HEAD_DIM), jnp.bfloat16)

    def pair_cols(p, base):
        return pl.ds(pl.multiple_of(base + p * 2 * HEAD_DIM, 2 * HEAD_DIM), 2 * HEAD_DIM)

    def beside(side, value, others):
        base = HEAD_DIM * (1 - side)
        result = zero
        for n, other in enumerate(others):
            result = jnp.where(lane == base + n, other, result)
        return jnp.where((lane < HEAD_DIM) if side == 0 else (lane >= HEAD_DIM), value, result)

    def attend(p, _):
        q = qkv[:, pair_cols(p, 0)]
        k = qkv[:, pair_cols(p, D)]
        v = qkv[:, pair_cols(p, 2 * D)]
        outs = []
        for side in range(2):
            s = mm(beside(side, q, [one]), beside(side, k, [penalty]), NT)
            top = jnp.max(s, -1, keepdims=True)
            s = jnp.exp(s - top)
            total = jnp.sum(s, -1, keepdims=True)
            logs[2 * p + side] = jnp.broadcast_to(top + jnp.log(total), (rows, 128))
            outs.append(mm(rounded(s * (1.0 / total)), v))
        o[:, pair_cols(p, 0)] = rounded(jnp.where(lane < HEAD_DIM, outs[0], outs[1]))
        return 0

    lax.fori_loop(0, HEADS // 2, attend, 0)
    ot[...] = o[...].T
    drain(wo, wsem.at[1])
    a[...] = mm(o[...], wo[...])
    for c in chunks:
        at = slice(c[0], c[0] + chunk)
        value = x_of(c) + (a[at, :] + vec(4))
        a[at, :] = value
        normed, _ = stats(value)
        n2[at, :] = rounded(normed * vec(5) + vec(6))
    n2t[...] = n2[...].T
    drain(wu, wsem.at[2])

    def up(i, _):
        cols = pl.ds(pl.multiple_of(i * WIDE, WIDE), WIDE)
        u = mm(n2[...], wu[:, cols]) + bias_up[:, cols]
        cumulative = 0.5 * (1.0 + lax.erf(u * 0.7071067811865476))
        hidden = rounded(u * cumulative)
        slope[:, cols] = cumulative + u * (jnp.exp(-0.5 * u * u) * 0.3989422804014327)
        h[:, cols] = hidden
        ht[cols, :] = hidden.T
        return 0

    lax.fori_loop(0, FF // WIDE, up, 0)
    drain(wd, wsem.at[3])
    y[...] = mm(h[...], wd[...])
    for c in chunks:
        at = slice(c[0], c[0] + chunk)
        value = a[at, :] + (y[at, :] + vec(11))
        y[at, :] = value
        normed, _ = stats(value)
        n3[at, :] = rounded(normed * vec(12) + vec(13))
    n3t[...] = n3[...].T
    drain(wp, wsem.at[4])
    keep = lax.broadcasted_iota(jnp.int32, (rows, 1), 0) < length
    z = jnp.where(keep, mm(n3[...], wp[...]) + vec(14), 0.0)
    if is_text:
        begin = MMROWS + IMG
        cat[:MMROWS, :] = vec_all[VECS : VECS + MMROWS, :]
        cat[MMROWS:begin, :] = zi_ref[0].astype(jnp.float32)
        cat[begin : begin + TXT, :] = z
        cat_ref[0] = rounded(cat[...])
    else:
        even = IMG // 16 * 16
        z_ref[0, :even, :] = rounded(z[:even])
        z_ref[0, even:IMG, :] = rounded(z[even:IMG])

    if not is_text:
        drain(grads, blank_sem)
    zeros = jnp.zeros((1, D), jnp.float32)
    total = zeros
    for c in chunks:
        at = slice(c[0], c[0] + chunk)
        g = jnp.where(keep[at, :], g_of(c), 0.0)
        total = total + jnp.sum(g, 0, keepdims=True)
        dyb[at, :] = rounded(g)
    vec_grad(14, total)
    put(1, square(6, mm(n3t[...], dyb[...])))
    dy[...] = mm(dyb[...], wp[...], NT)
    gain, shift, bias = zeros, zeros, zeros
    for c in chunks:
        at = slice(c[0], c[0] + chunk)
        normed, inverse = stats(y[at, :])
        g = dy[at, :]
        gain = gain + jnp.sum(g * normed, 0, keepdims=True)
        shift = shift + jnp.sum(g, 0, keepdims=True)
        g = norm_back(g * vec(12), normed, inverse)
        dy[at, :] = g
        low = rounded(g)
        dyb[at, :] = low
        bias = bias + jnp.sum(low.astype(jnp.float32), 0, keepdims=True)
    vec_grad(12, gain)
    vec_grad(13, shift)
    vec_grad(11, bias)

    def down(i, _):
        place = i % 2
        pl.when(i == 1)(functools.partial(free, 1, KB * KB))
        pl.when(i >= 2)(functools.partial(free, place, SET))
        cols = pl.ds(pl.multiple_of(i * WIDE, WIDE), WIDE)
        low = rounded(mm(dyb[...], wd[cols, :], NT) * slope[:, cols])
        du[:, cols] = low
        bias_up[:, cols] = jnp.sum(low.astype(jnp.float32), 0, keepdims=True)
        down_grad = mm(ht[cols, :], dyb[...])
        up_grad = mm(n2t[...], low)
        tiles = []
        for w in range(WIDE // T):
            band = slice(w * T, (w + 1) * T)
            number = i * (WIDE // T) + w
            for k in range(KB):
                other = slice(k * T, (k + 1) * T)
                tiles.append((starts[5] + number * KB + k, down_grad[band, other]))
                tiles.append((starts[4] + k * FB + number, up_grad[other, band]))
        put(place, tiles)
        return 0

    lax.fori_loop(0, FF // WIDE, down, 0)
    for i in range(FF // D):
        vec_grad(7 + i, bias_up[:, i * D : (i + 1) * D])
    da[...] = mm(du[...], wu[...], NT)
    gain, shift, bias = zeros, zeros, zeros
    for c in chunks:
        at = slice(c[0], c[0] + chunk)
        normed, inverse = stats(a[at, :])
        g = da[at, :]
        gain = gain + jnp.sum(g * normed, 0, keepdims=True)
        shift = shift + jnp.sum(g, 0, keepdims=True)
        g = dy[at, :] + norm_back(g * vec(5), normed, inverse)
        da[at, :] = g
        low = rounded(g)
        dab[at, :] = low
        bias = bias + jnp.sum(low.astype(jnp.float32), 0, keepdims=True)
    vec_grad(5, gain)
    vec_grad(6, shift)
    vec_grad(4, bias)
    dout = mm(dab[...], wo[...], NT)
    free(0, SET)
    put(0, square(3, mm(ot[...], dab[...])))
    low = rounded(dout)
    y[...] = low.astype(jnp.float32) * o[...].astype(jnp.float32)
    do[...] = low
    dot_[...] = low.T

    def attend_back(p, _):
        q = qkv[:, pair_cols(p, 0)]
        k = qkv[:, pair_cols(p, D)]
        v = qkv[:, pair_cols(p, 2 * D)]
        g = do[:, pair_cols(p, 0)]
        each = y[:, pair_cols(p, 0)]
        dqs, dks, dvs = [], [], []
        for side in range(2):
            half = pl.ds(pl.multiple_of((2 * p + side) * HEAD_DIM, HEAD_DIM), HEAD_DIM)
            mine = (lane < HEAD_DIM) if side == 0 else (lane >= HEAD_DIM)
            minus = [-one] * 3
            w = jnp.exp(
                mm(
                    beside(side, q, [one, *thirds(logs[2 * p + side])]),
                    beside(side, k, [penalty, *minus]),
                    NT,
                )
            )
            dvs.append(mm(dot_[half, :], rounded(w)))
            c = jnp.sum(jnp.where(mine, each, 0.0), -1, keepdims=True)
            dw = mm(
                beside(side, g, thirds(jnp.broadcast_to(c, (rows, 2 * HEAD_DIM)))),
                beside(side, v, minus),
                NT,
            )
            ds = rounded(w * dw)
            dqs.append(mm(ds, k))
            dks.append(mm(qt[half, :], ds))
        dqkv[:, pair_cols(p, 0)] = rounded(jnp.where(lane < HEAD_DIM, dqs[0], dqs[1]) * scale)
        dqkv[:, pair_cols(p, D)] = rounded(jnp.concatenate(dks, 0).T)
        dqkv[:, pair_cols(p, 2 * D)] = rounded(jnp.concatenate(dvs, 0).T)
        return 0

    lax.fori_loop(0, HEADS // 2, attend_back, 0)
    for m, number in ((0, 2), (2, 3)):
        vec_grad(number, jnp.sum(dqkv[:, m * D : (m + 1) * D].astype(jnp.float32), 0, keepdims=True))
    for m in range(3):
        free((1 + m) % 2, SET if m == 0 else KB * KB)
        put((1 + m) % 2, square(m, mm(n1t[...], dqkv[:, m * D : (m + 1) * D])))
    dy[...] = mm(dqkv[...], wqkv[...], NT)
    gain, shift = zeros, zeros
    for c in chunks:
        at = slice(c[0], c[0] + chunk)
        normed, inverse = stats(x_of(c))
        g = dy[at, :]
        gain = gain + jnp.sum(g * normed, 0, keepdims=True)
        shift = shift + jnp.sum(g, 0, keepdims=True)
        low = rounded(da[at, :] + norm_back(g * vec(0), normed, inverse))
        dx_ref[0, c[0] : c[1], :] = low[: c[1] - c[0]]
    vec_grad(0, gain)
    vec_grad(1, shift)
    if is_text:
        learned = cot_ref[0, :16, :].astype(jnp.float32)
        for i in range(MMROWS):
            vec_grad(VECS + i, learned[i : i + 1])
    free(0, KB * KB)
    free(1, KB * KB)
    drain(vec_out.at[pl.ds(0, vec_count)], vec_out_sem)


def tower(is_text, slots, tile_slot, lengths, x, cot, copies, before=()):
    bf, f32 = jnp.bfloat16, jnp.float32
    smem = pl.BlockSpec(memory_space=pltpu.SMEM)
    vmem = pl.BlockSpec(memory_space=pltpu.VMEM)
    hbm = pl.BlockSpec(memory_space=pl.ANY)
    dma = pltpu.SemaphoreType.DMA
    rows = -(-x.shape[1] // 16) * 16
    outs = [
        jax.ShapeDtypeStruct(cot.shape if is_text else x.shape, bf),
        jax.ShapeDtypeStruct(x.shape, bf),
        jax.ShapeDtypeStruct(copies.shape, bf),
    ]
    scratch = [
        pltpu.VMEM((D, 3 * D), bf), pltpu.VMEM((D, D), bf), pltpu.VMEM((D, FF), bf),
        pltpu.VMEM((FF, D), bf), pltpu.VMEM((D, D), bf),
        pltpu.VMEM((rows, D), bf), pltpu.VMEM((D, rows), bf),
        pltpu.VMEM((rows, 3 * D), bf), pltpu.VMEM((D, rows), bf),
        pltpu.VMEM((rows, D), bf), pltpu.VMEM((D, rows), bf),
        pltpu.VMEM((rows, D), f32),
        pltpu.VMEM((rows, D), bf), pltpu.VMEM((D, rows), bf),
        pltpu.VMEM((rows, FF), f32),
        pltpu.VMEM((rows, FF), bf), pltpu.VMEM((FF, rows), bf),
        pltpu.VMEM((rows, D), f32),
        pltpu.VMEM((rows, D), bf), pltpu.VMEM((D, rows), bf),
        pltpu.VMEM((cot.shape[1] if is_text else rows, D), f32),
        pltpu.VMEM((rows, D), f32),
        pltpu.VMEM((rows, 3 * D), bf),
        pltpu.VMEM((HEADS, rows, 128), f32),
        pltpu.VMEM((2, SET, T, T), bf),
        pltpu.VMEM((VECS + MMROWS, EXTRA, T), bf), pltpu.VMEM((VECS + MMROWS, D), f32),
        pltpu.VMEM((1, FF), f32), pltpu.VMEM((VECS + MMROWS, EXTRA, T), bf),
        dma((5,)), dma((2,)), dma, dma,
    ]
    if not is_text:
        scratch += [pltpu.VMEM((slots * T + EXTRA, T), bf), dma]
    return pl.pallas_call(
        functools.partial(tower_body, is_text, rows, slots),
        in_specs=[smem, smem, vmem, vmem, hbm] + ([vmem, hbm] if is_text else []),
        out_specs=[vmem, vmem, hbm],
        out_shape=outs,
        scratch_shapes=scratch,
        input_output_aliases={6: 2} if is_text else {},
        compiler_params=pltpu.CompilerParams(vmem_limit_bytes=63 << 20),
        name="text_tower" if is_text else "image_tower",
    )(tile_slot, lengths, x, cot, copies, *before)


def split(x):
    hi = x.astype(jnp.bfloat16)
    lo = (x - hi.astype(jnp.float32)).astype(jnp.bfloat16)
    return hi, lo


def dot(a, b, dims):
    return lax.dot_general(a, b, dims, preferred_element_type=jnp.float32)


def mm3(a, b, dims):
    return dot(a[0], b[0], dims) + (dot(a[0], b[1], dims) + dot(a[1], b[0], dims))


def adam_step(first, second):
    return (
        first
        / (1.0 - BETA_ONE**STEP)
        / (jnp.sqrt(second / (1.0 - BETA_TWO**STEP)) + EPSILON)
    )


def refine(i, slots, g_ref, w_ref, m1_ref, m2_ref, ls_ref, rs_ref, lb_ref, rb_ref,
           wn_ref, m1n_ref, m2n_ref, lsn_ref, rsn_ref, work):
    e = split(g_ref[...])
    ql = split(lb_ref[0])
    qr = split(rb_ref[0])
    left = BETA_TWO * ls_ref[0] + (1.0 - BETA_TWO) * mm3(e, e, NT)
    right = BETA_TWO * rs_ref[0] + (1.0 - BETA_TWO) * mm3(e, e, TN)
    lsn_ref[0] = left
    rsn_ref[0] = right
    turned = mm3(split(mm3(ql, e, TN)), qr, NN)
    first = BETA_ONE * m1_ref[0] + (1.0 - BETA_ONE) * turned
    second = BETA_TWO * m2_ref[0] + (1.0 - BETA_TWO) * turned * turned
    m1n_ref[0] = first
    m2n_ref[0] = second
    direction = mm3(split(mm3(ql, split(adam_step(first, second)), NN)), qr, NT)
    w = w_ref[0]
    wn_ref[0] = w - RATE_MATRIX * (direction + DECAY * w)
    for side, (basis, stat) in enumerate(((ql, left), (qr, right))):
        y = mm3(basis, split(stat), TN)
        y = y * lax.rsqrt(jnp.sum(y * y, axis=1, keepdims=True))
        work[side * slots + i, :, T:] = y
        y = split(y)
        work[side * slots + i, :, :T] = mm3(y, y, NT)


B = 64
GROUP = 8
ABREAST = 4


def eliminate(count, diag):
    shape = (GROUP, 2 * B)
    subs = lax.broadcasted_iota(jnp.int32, shape, 0)
    for jg in range(B // GROUP):
        top = slice(jg * GROUP, jg * GROUP + GROUP)
        tops = [diag[m, top, :] for m in range(count)]
        for jj in range(0, GROUP, 2):
            j = jg * GROUP + jj
            for m in range(count):
                tile = tops[m]
                first = jnp.broadcast_to(tile[:, j : j + 1], shape)
                second = jnp.broadcast_to(tile[:, j + 1 : j + 2], shape)
                p00, p01, p11 = first[jj : jj + 1], second[jj : jj + 1], second[jj + 1 : jj + 2]
                r0, r1 = tile[jj : jj + 1], tile[jj + 1 : jj + 2]
                inverse = 1.0 / (p00 * p11 - p01 * p01)
                cross = p01 * inverse
                t0 = (p11 * inverse) * r0 - cross * r1
                t1 = (p00 * inverse) * r1 - cross * r0
                lower = tile - first * t0 - second * t1
                tops[m] = jnp.where(
                    subs > jj + 1, lower, jnp.where(subs == jj + 1, tile - (p01 / p00) * r0, tile)
                )
                if jg < B // GROUP - 1:
                    rest = diag[m, jg * GROUP + GROUP :, :]
                    diag[m, jg * GROUP + GROUP :, :] = (
                        rest - rest[:, j : j + 1] * t0 - rest[:, j + 1 : j + 2] * t1
                    )
        for m in range(count):
            diag[m, top, :] = tops[m]


def orthonormal(count, work, diag):
    row = lax.broadcasted_iota(jnp.int32, (B, 2 * B), 0)
    lane = lax.broadcasted_iota(jnp.int32, (B, 2 * B), 1)
    def load(k):
        low = k * B
        edge = low // (2 * B) * 2 * B
        for m in range(count):
            block = work[m, low : low + B, edge : edge + 2 * B]
            if low % (2 * B):
                block = pltpu.roll(block, B, 1)
            diag[m] = jnp.where(lane < B, block, jnp.where(lane == row + B, 1.0, 0.0))

    def products(k):
        low = k * B
        edge = low // (2 * B) * 2 * B

        def apply(step, _):
            for n in range(ABREAST):
                m = step * ABREAST + n
                d = diag[m]
                pivots = jnp.sum(jnp.where(lane == row, d, 0.0), axis=1, keepdims=True)
                high, rest = split(d[:, B:] * lax.rsqrt(pivots))
                inverse = jnp.concatenate([high, rest, high], 1)
                high, rest = split(work[m, low : low + B, edge:])
                new = dot(inverse, jnp.concatenate([high, high, rest], 0), NN)
                work[m, low : low + B, edge:] = new
                if low + B < T:
                    high, rest = split(new)
                    after = low + B - edge
                    begin = (low + B) // (2 * B) * 2 * B
                    left = jnp.concatenate([high, rest, high], 0)[:, after : T - edge]
                    right = jnp.concatenate([high, high, rest], 0)[:, begin - edge :]
                    work[m, low + B :, begin:] = work[m, low + B :, begin:] - dot(left, right, TN)
            return 0

        lax.fori_loop(0, count // ABREAST, apply, 0)

    def block(k, _):
        for which in range(T // B):
            pl.when(k == which)(functools.partial(load, which))
        eliminate(count, diag)
        for which in range(T // B):
            pl.when(k == which)(functools.partial(products, which))
        return 0

    lax.fori_loop(0, T // B, block, 0)


def optimizer_body(slots, g_ref, vg_ref, w_ref, m1_ref, m2_ref, ls_ref, rs_ref, lb_ref, rb_ref, vw_ref, v1_ref, v2_ref,
                   wn_ref, m1n_ref, m2n_ref, lsn_ref, rsn_ref, lbn_ref, rbn_ref, vwn_ref, v1n_ref, v2n_ref, work, diag):
    i = pl.program_id(0)

    @pl.when(i == 0)
    def _():
        for k in range(vw_ref.shape[1] // T):
            cols = slice(k * T, (k + 1) * T)
            g = vg_ref[k : k + 1, :]
            first = BETA_ONE * v1_ref[:, cols] + (1.0 - BETA_ONE) * g
            second = BETA_TWO * v2_ref[:, cols] + (1.0 - BETA_TWO) * g * g
            v1n_ref[:, cols] = first
            v2n_ref[:, cols] = second
            vwn_ref[:, cols] = vw_ref[:, cols] - RATE_VECTOR * adam_step(first, second)

    refine(i, slots, g_ref, w_ref, m1_ref, m2_ref, ls_ref, rs_ref, lb_ref, rb_ref,
           wn_ref, m1n_ref, m2n_ref, lsn_ref, rsn_ref, work)

    @pl.when(i == slots - 1)
    def _():
        orthonormal(work.shape[0], work, diag)

        def finish(m, _):
            lbn_ref[m] = work[m, :, T:].T
            rbn_ref[m] = work[slots + m, :, T:].T
            return 0

        lax.fori_loop(0, slots, finish, 0)


def optimizer(g, w, m1, m2, ls, rs, lb, rb, vw, v1, v2):
    slots = w.shape[0]
    count = -(-2 * slots // ABREAST) * ABREAST
    one = pl.BlockSpec((1, T, T), lambda i: (i, 0, 0))
    every = pl.BlockSpec((slots, T, T), lambda i: (0, 0, 0))
    line = pl.BlockSpec(vw.shape, lambda i: (0, 0))
    f32 = jnp.float32
    return pl.pallas_call(
        functools.partial(optimizer_body, slots),
        grid=(slots,),
        in_specs=[
            pl.BlockSpec((T, T), lambda i: (i, 0)),
            pl.BlockSpec((EXTRA, T), lambda i: (slots * T // EXTRA, 0)),
        ]
        + [one] * 7
        + [line] * 3,
        out_specs=[one] * 5 + [every] * 2 + [line] * 3,
        out_shape=[jax.ShapeDtypeStruct(w.shape, f32)] * 7 + [jax.ShapeDtypeStruct(vw.shape, f32)] * 3,
        scratch_shapes=[
            pltpu.VMEM((count, T, 2 * T), f32),
            pltpu.VMEM((count, B, 2 * B), f32),
        ],
        compiler_params=pltpu.CompilerParams(vmem_limit_bytes=60 << 20),
        name="optimizer",
    )(g, g, w, m1, m2, ls, rs, lb, rb, vw, v1, v2)


ORDERS = ("xzy", "yzx", "zxy", "zyx")


def part_rows(slots):
    quarter = slots * T // 4
    sizes = [quarter, quarter, quarter, quarter + EXTRA]
    return [(sum(sizes[:i]), sizes[i]) for i in range(4)]


def last_step(order, key):
    away = {"z": key[0], "x": key[1], "y": key[2]}
    steps = [i for i in range(3) if away[order[i]]]
    return steps[-1] if steps else -1


def plan_of(depth):
    cells = list(itertools.product(range(depth), range(2), range(2)))
    queues, free, events, arrived = {}, {}, [], {}
    ticket = itertools.count()

    def onward(cell, part, source, now):
        order = ORDERS[part]
        key = (source[0] - cell[0], source[1] ^ cell[1], source[2] ^ cell[2])
        step = last_step(order, key)
        for i in range(3):
            z, x, y = cell
            if order[i] == "z":
                if i > step:
                    ways = (1, -1)
                elif i == step:
                    ways = (1,) if key[0] < 0 else (-1,)
                else:
                    ways = ()
                targets = [(z + w, x, y) for w in ways if 0 <= z + w < depth]
            elif i > step:
                targets = [(z, 1 - x, y) if order[i] == "x" else (z, x, 1 - y)]
            else:
                targets = []
            for target in targets:
                heapq.heappush(queues.setdefault((cell, target), []), (now, next(ticket), part, source))
                heapq.heappush(events, (now, next(ticket), 0, (cell, target)))

    for cell in cells:
        for part in range(4):
            onward(cell, part, cell, 0.0)
    while events:
        now, _, kind, what = heapq.heappop(events)
        if kind == 0:
            if queues[what] and free.get(what, 0.0) <= now:
                _, _, part, source = heapq.heappop(queues[what])
                free[what] = now + 2.0
                heapq.heappush(events, (now + 2.0, next(ticket), 0, what))
                heapq.heappush(events, (now + 2.5, next(ticket), 1, (what[1], part, source)))
        else:
            cell, part, source = what
            key = (part, source[0] - cell[0], source[1] ^ cell[1], source[2] ^ cell[2])
            arrived.setdefault(key, []).append(now)
            onward(cell, part, source, now)
    times = {k: sum(v) / len(v) for k, v in arrived.items()}
    fixed = {}

    def time_of(key):
        if key not in fixed:
            part, dz, dx, dy = key
            step = last_step(ORDERS[part], key[1:])
            if step < 0:
                return 0.0
            dim = ORDERS[part][step]
            if dim == "z":
                parent = (part, dz - (1 if dz > 0 else -1), dx, dy)
            else:
                parent = (part, dz, 0 if dim == "x" else dx, 0 if dim == "y" else dy)
            fixed[key] = max(times[key], time_of(parent) + 0.01)
        return fixed[key]

    return sorted(times, key=lambda k: (time_of(k), k))


class Place:
    def __init__(self, depth):
        tower = lax.axis_index("tower")
        self.depth = depth
        self.core = tower % 2
        self.x = tower // 2 % 2
        self.z = tower // 4
        self.y = lax.axis_index("batch")

    def at(self, dz=0, dx=0, dy=0):
        return (
            self.z + dz,
            1 - self.x if dx else self.x,
            1 - self.y if dy else self.y,
        )

    def device(self, cell, other=False):
        core = 1 - self.core if other else self.core
        return ((cell[0] * 2 + cell[1]) * 2 + core, cell[2])

    def block(self, cell, other=False):
        core = 1 - self.core if other else self.core
        return ((cell[0] * 2 + cell[1]) * 2 + core) * 2 + cell[2]

    def spot(self, cell):
        return (cell[0] * 2 + cell[1]) * 2 + cell[2]

    def inside(self, dz):
        if dz == 0:
            return None
        return self.z + dz < self.depth if dz > 0 else self.z + dz >= 0

    def meet(self):
        barrier = pltpu.get_barrier_semaphore()

        def greet(device):
            pl.semaphore_signal(barrier, inc=1, device_id=device, device_id_type=pl.DeviceIdType.MESH)

        greet(self.device(self.at(), True))
        greet(self.device(self.at(dx=1)))
        greet(self.device(self.at(dy=1)))
        for way in (1, -1):
            pl.when(self.inside(way))(functools.partial(greet, self.device(self.at(dz=way))))
        low = (self.z > 0).astype(jnp.int32)
        high = (self.z < self.depth - 1).astype(jnp.int32)
        pl.semaphore_wait(barrier, 3 + low + high)


def guarded(conditions, action):
    conditions = [c for c in conditions if c is not None]
    if not conditions:
        action()
    else:
        both = conditions[0]
        for c in conditions[1:]:
            both = jnp.logical_and(both, c)
        pl.when(both)(action)


def remote(src, dst, send, recv, device):
    return pltpu.make_async_remote_copy(
        src_ref=src, dst_ref=dst, send_sem=send, recv_sem=recv,
        device_id=device, device_id_type=pl.DeviceIdType.MESH,
    )


def drain(ref, sem):
    pltpu.make_async_copy(ref, ref, sem).wait()


def gather_body(
    depth, parts, plan, tiles_ref, vec_ref, out_ref, wide, own_ref, wide_sem, own_sem, z_sem, flat_sem, twin_sem, recv_sem
):
    slots = tiles_ref.shape[0]
    for slot in range(slots):
        pltpu.make_async_copy(tiles_ref.at[slot], wide.at[slot], wide_sem.at[slot]).start()
    here = Place(depth)
    here.meet()
    line = vec_ref[...].astype(jnp.bfloat16)
    pieces = [line[:, k * T : (k + 1) * T] for k in range(line.shape[1] // T)]
    pieces.append(jnp.zeros((EXTRA - len(pieces), T), jnp.bfloat16))
    own_ref[slots * T :, :] = jnp.concatenate(pieces, 0)
    for slot in range(slots):
        drain(wide.at[slot], wide_sem.at[slot])
        own_ref[slot * T : (slot + 1) * T, :] = wide[slot].astype(jnp.bfloat16)
    mine = pltpu.make_async_copy(own_ref, out_ref.at[here.block(here.at())], own_sem)
    mine.start()
    waits = []

    def handle(part, key):
        start, size = parts[part]
        rows = pl.ds(start, size)
        order = ORDERS[part]
        step = last_step(order, key)
        cell = here.at(*key)
        present = here.inside(key[0])
        block = here.block(cell)
        spot = here.spot(cell)
        place = out_ref.at[block, rows]
        source = own_ref.at[rows] if step < 0 else place

        def arrive():
            if step >= 0:
                drain(place, recv_sem.at[part, spot])

        guarded([present], arrive)
        for i in range(3):
            dim = order[i]
            if dim == "z":
                ways = (1, -1) if i > step else ()
                if i == step:
                    ways = (1,) if key[0] < 0 else (-1,)
                for way in ways:
                    sem = z_sem.at[part, spot, 0 if way > 0 else 1]
                    copy = remote(source, place, sem, recv_sem.at[part, spot], here.device(here.at(dz=way)))
                    conditions = [present, here.inside(way)]
                    guarded(conditions, copy.start)
                    waits.append((conditions, copy.wait_send))
            elif i > step:
                target = here.at(dx=1) if dim == "x" else here.at(dy=1)
                guarded(
                    [present],
                    remote(
                        source, place, flat_sem.at[part, 0 if dim == "x" else 1],
                        recv_sem.at[part, spot], here.device(target),
                    ).start,
                )
        guarded(
            [present],
            remote(source, place, twin_sem.at[0], twin_sem.at[1], here.device(here.at(), True)).start,
        )

    for part in range(4):
        handle(part, (0, 0, 0))
    for part, *key in plan:
        handle(part, tuple(key))
    for conditions, action in waits:
        guarded(conditions, action)
    for part in range(4):
        rows = pl.ds(*parts[part])
        sent = 1
        for dim in ORDERS[part]:
            if dim != "z":
                drain(out_ref.at[pl.ds(0, sent), rows], flat_sem.at[part, 0 if dim == "x" else 1])
            sent *= depth if dim == "z" else 2
    mine.wait()
    half = pl.ds(0, 4 * depth)
    drain(out_ref.at[half], twin_sem.at[0])
    drain(out_ref.at[half], twin_sem.at[1])


def gather(depth, tiles, vec):
    slots = tiles.shape[0]
    parts = part_rows(slots)
    rows = slots * T + EXTRA
    hbm = pl.BlockSpec(memory_space=pl.ANY)
    dma = pltpu.SemaphoreType.DMA
    return pl.pallas_call(
        functools.partial(gather_body, depth, parts, plan_of(depth)),
        in_specs=[hbm, pl.BlockSpec(memory_space=pltpu.VMEM)],
        out_specs=hbm,
        out_shape=jax.ShapeDtypeStruct((8 * depth, rows, T), jnp.bfloat16),
        scratch_shapes=[
            pltpu.VMEM(tiles.shape, jnp.float32),
            pltpu.VMEM((rows, T), jnp.bfloat16),
            dma((slots,)),
            dma,
            dma((4, 4 * depth, 2)),
            dma((4, 2)),
            dma((2,)),
            dma((4, 4 * depth)),
        ],
        compiler_params=pltpu.CompilerParams(
            collective_id=0, has_side_effects=True, vmem_limit_bytes=60 << 20
        ),
        name="gather",
    )(tiles, vec)


def add_rows(size, target, start, sources):
    def piece(at, count):
        total = sources[0][pl.ds(at, count), :].astype(jnp.float32)
        for source in sources[1:]:
            total = total + source[pl.ds(at, count), :].astype(jnp.float32)
        target[pl.ds(start + at, count), :] = total.astype(target.dtype)

    whole = size // 128

    def body(i, _):
        piece(pl.multiple_of(i * 128, 128), 128)
        return 0

    lax.fori_loop(0, whole, body, 0)
    if size % 128:
        piece(whole * 128, size % 128)


def reduce_body(depth, parts, plan, grads_ref, out_ref, acc, twin, flat0, flat1, line, *sems):
    load_sem, twin_send, twin_recv, flat0_send, flat0_recv, flat1_send, flat1_recv, line_send, line_recv = sems
    here = Place(depth)
    keys = [(part, tuple(key)) for part, *key in reversed(plan)] + [(part, (0, 0, 0)) for part in range(4)]
    loads = []
    for part, key in keys:
        if key not in loads:
            loads.append(key)
    for key in loads:
        cell = here.at(*key)
        guarded(
            [here.inside(key[0])],
            pltpu.make_async_copy(
                grads_ref.at[here.block(cell)], acc.at[here.spot(cell)], load_sem.at[here.spot(cell)]
            ).start,
        )
    here.meet()
    other = here.device(here.at(), True)
    for part, key in keys:
        cell = here.at(*key)
        rows = pl.ds(*parts[part])
        spot = here.spot(cell)
        guarded(
            [here.inside(key[0])],
            remote(
                grads_ref.at[here.block(cell, True), rows], twin.at[spot, rows], twin_send,
                twin_recv.at[part, spot], other,
            ).start,
        )
    for end, shift in ((0, 1), (depth - 1, 0)):

        def clear():
            for part in range(4):
                columns = 2 if ORDERS[part][1] == "z" else 1
                for column in range(columns):
                    for target in range(depth):
                        place = line.at[part, column, target + shift]
                        place[...] = jnp.zeros(place.shape, place.dtype)

        pl.when(here.z == end)(clear)
    waits = []
    loaded = set()
    for part, key in keys:
        start, size = parts[part]
        rows = pl.ds(start, size)
        short = pl.ds(0, size)
        first, second, third = reversed(ORDERS[part])
        away = {"z": key[0], "x": key[1], "y": key[2]}
        cell = here.at(*key)
        spot = here.spot(cell)
        present = here.inside(key[0])
        step = last_step(ORDERS[part], key)
        index0 = cell[0] * 2 + (cell[1] if first == "y" else cell[2])

        def task(part=part, key=key, start=start, size=size, rows=rows, short=short, step=step, cell=cell,
                 spot=spot, first=first, second=second, third=third, away=away, index0=index0):
            if key not in loaded:
                drain(acc.at[spot], load_sem.at[spot])
            drain(twin.at[spot, rows], twin_recv.at[part, spot])
            mine = acc.at[spot, rows]
            sources = [mine, twin.at[spot, rows]]
            order = ORDERS[part]
            column = 0
            if order[1] == "z":
                column = cell[1] if order[0] == "x" else cell[2]
            for i in (2, 1, 0):
                if i <= step - 1 or (i == step and order[i] != "z"):
                    break
                if i == 2 and order[i] != "z":
                    drain(flat0.at[part, index0, short], flat0_recv.at[part, index0])
                    sources.append(flat0.at[part, index0, short])
                elif order[i] != "z":
                    which = cell[0] if i == 1 else 0
                    drain(flat1.at[part, which, short], flat1_recv.at[part, which])
                    sources.append(flat1.at[part, which, short])
                else:
                    ways = (1, 0)
                    if i == step:
                        ways = (1,) if key[0] > 0 else (0,)
                    for way in ways:
                        place = line.at[part, column, cell[0] + way, short]

                        def arrive(place=place, way=way):
                            drain(place, line_recv.at[part, column, cell[0] + way])

                        pl.when(here.z > 0 if way else here.z < depth - 1)(arrive)
                        sources.append(place)
                    if i == step:
                        break
            if step < 0:
                add_rows(size, out_ref, start, sources)
                return
            add_rows(size, acc.at[spot], start, sources)
            dim = order[step]
            if dim == "z":
                way = 1 if key[0] > 0 else 0
                remote(
                    mine, line.at[part, column, cell[0] + way, short], line_send.at[part, column, cell[0]],
                    line_recv.at[part, column, cell[0] + way], here.device(here.at(dz=1 if way else -1)),
                ).start()
                return
            target = here.device(here.at(dx=1) if dim == "x" else here.at(dy=1))
            if step == 2:
                remote(
                    mine, flat0.at[part, index0, short], flat0_send.at[part], flat0_recv.at[part, index0], target
                ).start()
            else:
                which = cell[0] if step == 1 else 0
                remote(
                    mine, flat1.at[part, which, short], flat1_send.at[part], flat1_recv.at[part, which], target
                ).start()

        guarded([present], task)
        loaded.add(key)
        if step >= 0 and ORDERS[part][step] == "z":
            column = 0
            if ORDERS[part][1] == "z":
                column = cell[1] if ORDERS[part][0] == "x" else cell[2]
            waits.append(
                ([present], functools.partial(drain, acc.at[spot, rows], line_send.at[part, column, cell[0]]))
            )
    for conditions, action in waits:
        guarded(conditions, action)
    for part in range(4):
        rows = pl.ds(*parts[part])
        order = ORDERS[part]
        sent = 1
        for i, dim in enumerate(order):
            if dim != "z":
                sem = flat0_send if i == 2 else flat1_send
                drain(acc.at[pl.ds(0, sent), rows], sem.at[part])
            sent *= depth if dim == "z" else 2
    drain(acc, twin_send)


def reduce_blocks(depth, slots, grads):
    parts = part_rows(slots)
    rows = grads.shape[1]
    longest = max(size for _, size in parts)
    dma = pltpu.SemaphoreType.DMA
    bf = jnp.bfloat16
    return pl.pallas_call(
        functools.partial(reduce_body, depth, parts, plan_of(depth)),
        in_specs=[pl.BlockSpec(memory_space=pl.ANY)],
        out_specs=pl.BlockSpec(memory_space=pltpu.VMEM),
        out_shape=jax.ShapeDtypeStruct((rows, T), jnp.float32),
        scratch_shapes=[
            pltpu.VMEM((4 * depth, rows, T), bf),
            pltpu.VMEM((4 * depth, rows, T), bf),
            pltpu.VMEM((4, 2 * depth, longest, T), bf),
            pltpu.VMEM((4, depth, longest, T), bf),
            pltpu.VMEM((4, 2, depth + 1, longest, T), bf),
            dma((4 * depth,)),
            dma,
            dma((4, 4 * depth)),
            dma((4,)),
            dma((4, 2 * depth)),
            dma((4,)),
            dma((4, depth)),
            dma((4, 2, depth)),
            dma((4, 2, depth + 1)),
        ],
        compiler_params=pltpu.CompilerParams(
            collective_id=1, has_side_effects=True, vmem_limit_bytes=63 << 20
        ),
        name="reduce_blocks",
    )(grads)


def grid_depth():
    towers = lax.axis_size("tower")
    if lax.axis_size("batch") != 2 or towers % 4 or towers > 16 or towers < 8:
        return None
    return towers // 4


def all_blocks(tiles, vec):
    depth = grid_depth()
    if depth is not None:
        return gather(depth, tiles, vec)
    own = jnp.concatenate([tiles.reshape(-1, T), vec.reshape(-1, T)], 0)
    own = jnp.pad(own, ((0, EXTRA - vec.size // T), (0, 0))).astype(jnp.bfloat16)
    return lax.all_gather(own, ("tower", "batch"), axis=0)


def own_sums(slots, grads):
    depth = grid_depth()
    if depth is not None:
        return reduce_blocks(depth, slots, grads)
    return lax.psum_scatter(grads, ("tower", "batch"), scatter_dimension=0).astype(jnp.float32)


def per_device(
    image_rows,
    text_rows,
    caption_lengths,
    concat_cot,
    tile_slot,
    tile_weight,
    tile_first,
    tile_second,
    left_stat,
    right_stat,
    left_basis,
    right_basis,
    vec_weight,
    vec_first,
    vec_second,
):
    slots = tile_weight.shape[0]
    copies = all_blocks(tile_weight, vec_weight)
    projected, image_grad, grads = tower(
        False, slots, tile_slot, caption_lengths, image_rows, concat_cot, copies
    )
    concat, text_grad, grads = tower(
        True, slots, tile_slot, caption_lengths, text_rows, concat_cot, copies, (projected, grads)
    )
    states = optimizer(
        own_sums(slots, grads),
        tile_weight,
        tile_first,
        tile_second,
        left_stat,
        right_stat,
        left_basis,
        right_basis,
        vec_weight,
        vec_first,
        vec_second,
    )
    return (concat, image_grad, text_grad, *states)


def solution(mesh):
    return jax.shard_map(
        per_device,
        mesh=mesh,
        in_specs=(
            P(("tower", "batch"), None, None),
            P(("tower", "batch"), None, None),
            P(),
            P(("tower", "batch"), None, None),
            P(),
            P(("tower", "batch"), None, None),
            P(("tower", "batch"), None, None),
            P(("tower", "batch"), None, None),
            P(("tower", "batch"), None, None),
            P(("tower", "batch"), None, None),
            P(("tower", "batch"), None, None),
            P(("tower", "batch"), None, None),
            P(("tower", "batch"), None),
            P(("tower", "batch"), None),
            P(("tower", "batch"), None),
        ),
        out_specs=(
            P(("tower", "batch"), None, None),
            P(("tower", "batch"), None, None),
            P(("tower", "batch"), None, None),
            P(("tower", "batch"), None, None),
            P(("tower", "batch"), None, None),
            P(("tower", "batch"), None, None),
            P(("tower", "batch"), None, None),
            P(("tower", "batch"), None, None),
            P(("tower", "batch"), None, None),
            P(("tower", "batch"), None, None),
            P(("tower", "batch"), None),
            P(("tower", "batch"), None),
            P(("tower", "batch"), None),
        ),
        check_vma=False,
    )
```

time: 3530 us -> 441 us (0.12)
  waiting for transfers between devices: 1450 us -> 0 us
  other arithmetic: 1020 us -> 0 us
  local copies, waits for them, and re-layouts: 536 us -> 0 us
  Pallas kernels: 0 us -> 438 us
  matrix products: 280 us -> 0 us
  blocking collectives: 171 us -> 0 us
  loops' own time: 36.1 us -> 0 us
    reduce_scatter x1 -> x0, waiting for transfers between devices: 1330 us -> none  [per_device(): lax.psum_scatter(tile_terms, ('tower', 'batch'), scatter_dimension=0, til...]
    another operation x19 -> x0, other arithmetic: 864 us -> none  [the longest x14 543 us: orthonormal(): lower_factor = jnp.linalg.cholesky(gram_matrix)]
    pallas_call x0 -> x5, Pallas kernels: none -> 438 us  [the longest x1 137 us: reduce_blocks(): pl.pallas_call(functools.partial(reduce_body, depth, parts, plan_of(depth...]
    dot_general x64 -> x0, matrix products: 255 us -> none  [the longest x14 78.2 us: apply_weight(): return jnp.dot(left_rows, matrix, preferred_element_type=jnp.float32)]
    all_gather x1 -> x0, blocking collectives: 171 us -> none  [per_device(): lax.all_gather(vec_weight.astype(jnp.bfloat16), ('tower', 'batch'), axis=...]
    scatter x3 -> x0, local copies, waits for them, and re-layouts: 111 us -> none  [the longest x2 111 us: per_device(): tile_terms = tile_terms.at[my_slots].set(tiles_from(outcome[4]))]
    reshape x23 -> x0, local copies, waits for them, and re-layouts: 110 us -> none  [the longest x14 93.8 us: tiles_of(): matrix.reshape(rows_count // TILE_ORDER, TILE_ORDER, cols_count // TILE_O...]
    transpose x14 -> x0, local copies, waits for them, and re-layouts: 87.3 us -> none  [tiles_of(): return blocks.transpose(0, 2, 1, 3).reshape(-1, TILE_ORDER, TILE_ORDER)]
  transfers between devices with their start and end apart: 7 -> 0, of which waited for: 4 -> 0; matrix products, arithmetic and copies ran while one was open for 17% -> 0% of each run, Pallas kernels for 0% -> 0%
where the time goes in v1:
time: 441 us; the launch traced here: 439 us
  Pallas kernels  438 us (99%)
    pallas_call x1, Pallas kernels, reduce_blocks(): pl.pallas_call(functools.partial(reduce_body, depth, parts, plan_of(depth...  137 us
    pallas_call x1, Pallas kernels, gather(): pl.pallas_call(functools.partial(gather_body, depth, parts, plan_of(depth...  127 us
    pallas_call x2, Pallas kernels, tower(): pl.pallas_call(functools.partial(tower_body, is_text, rows, slots), in_sp...  103 us
    pallas_call x1, Pallas kernels, optimizer(): pl.pallas_call(functools.partial(optimizer_body, slots), grid=(slots,), i...  70.9 us

profile of v1, /device:TPU:18, one launch (start us, length us, event | category | flops | bytes accessed | tf_op | source)
XLA Modules:
  0.0 438.5 jit_solution(1931835045808912172)
XLA Ops:
  0.6 127.0 %gather.1.copies = bf16[32,2064,256]{2,1,0:T(8,128)(2,1)} custom-call(f32[8,256,256]{2,1,0:T(8,128)} %w_ref.1, f32[1,768]{1,0:T(1,128)} %vw_ref.1), custom_call_target="tpu_custom_call" | custom-call | tf_op jit(solution)/shard_map/gather/pallas_call | solution.py:879
  127.7 39.5 %image_tower.1 = (bf16[1,197,768]{2,1,0:T(8,128)(2,1)}, bf16[1,197,768]{2,1,0:T(8,128)(2,1)}, bf16[32,2064,256]{2,1,0:T(8,128)(2,1)}) custom-call(s32[234]{0:T(256)} %slot_ref.3, s32[32]{0:T(128)} %length_ref.3, bf16[1,197,768]{2,1,0:T(8,128)(2,1)} %x_ref.2, bf16[1,711,768]{2,1,0:T(8,128)(2,1)} %cot_ref.3, bf16[32,2064,256]{2,1,0:T(8,128)(2,1)} %gather.1.copies), custom_call_target="tpu_custom_call" | custom-call | tf_op jit(solution)/shard_map/image_tower/pallas_call | solution.py:444
  167.1 63.5 %text_tower.1 = (bf16[1,711,768]{2,1,0:T(8,128)(2,1)}, bf16[1,512,768]{2,1,0:T(8,128)(2,1)}, bf16[32,2064,256]{2,1,0:T(8,128)(2,1)}) custom-call(s32[234]{0:T(256)} %slot_ref.3, s32[32]{0:T(128)} %length_ref.3, bf16[1,512,768]{2,1,0:T(8,128)(2,1)} %x_ref.3, bf16[1,711,768]{2,1,0:T(8,128)(2,1)} %cot_ref.3, ...), custom_call_target="tpu_custom_call", output_to_operand_aliasing={{2}: (6, {})} | custom-call | tf_op jit(solution)/shard_map/text_tower/pallas_call | solution.py:444
  230.6 136.8 %reduce_blocks.1.g_ref.vg_ref = f32[2064,256]{1,0:T(8,128)} custom-call(bf16[32,2064,256]{2,1,0:T(8,128)(2,1)} %get-tuple-element.34.grads_ref), custom_call_target="tpu_custom_call" | custom-call | tf_op jit(solution)/shard_map/reduce_blocks/pallas_call | solution.py:1060
  367.4 70.9 %optimizer.1 = (f32[8,256,256]{2,1,0:T(8,128)}, f32[8,256,256]{2,1,0:T(8,128)}, f32[8,256,256]{2,1,0:T(8,128)}, f32[8,256,256]{2,1,0:T(8,128)}, f32[8,256,256]{2...) custom-call(f32[2064,256]{1,0:T(8,128)} %reduce_blocks.1.g_ref.vg_re, ...), custom_call_target="tpu_custom_call" | custom-call | tf_op jit(solution)/shard_map/optimizer/pallas_call | solution.py:624

commit v2 on v1

--- a/solution.py
+++ b/solution.py
@@ -475,170 +475,218 @@
     )
 
 
-def refine(i, slots, g_ref, w_ref, m1_ref, m2_ref, ls_ref, rs_ref, lb_ref, rb_ref,
-           wn_ref, m1n_ref, m2n_ref, lsn_ref, rsn_ref, work):
-    e = split(g_ref[...])
-    ql = split(lb_ref[0])
-    qr = split(rb_ref[0])
-    left = BETA_TWO * ls_ref[0] + (1.0 - BETA_TWO) * mm3(e, e, NT)
-    right = BETA_TWO * rs_ref[0] + (1.0 - BETA_TWO) * mm3(e, e, TN)
-    lsn_ref[0] = left
-    rsn_ref[0] = right
-    turned = mm3(split(mm3(ql, e, TN)), qr, NN)
-    first = BETA_ONE * m1_ref[0] + (1.0 - BETA_ONE) * turned
-    second = BETA_TWO * m2_ref[0] + (1.0 - BETA_TWO) * turned * turned
-    m1n_ref[0] = first
-    m2n_ref[0] = second
-    direction = mm3(split(mm3(ql, split(adam_step(first, second)), NN)), qr, NT)
-    w = w_ref[0]
-    wn_ref[0] = w - RATE_MATRIX * (direction + DECAY * w)
-    for side, (basis, stat) in enumerate(((ql, left), (qr, right))):
-        y = mm3(basis, split(stat), TN)
-        y = y * lax.rsqrt(jnp.sum(y * y, axis=1, keepdims=True))
-        work[side * slots + i, :, T:] = y
-        y = split(y)
-        work[side * slots + i, :, :T] = mm3(y, y, NT)
-
-
 B = 64
 GROUP = 8
-ABREAST = 4
-
-
-def eliminate(count, diag):
-    shape = (GROUP, 2 * B)
-    subs = lax.broadcasted_iota(jnp.int32, shape, 0)
-    for jg in range(B // GROUP):
-        top = slice(jg * GROUP, jg * GROUP + GROUP)
-        tops = [diag[m, top, :] for m in range(count)]
-        for jj in range(0, GROUP, 2):
-            j = jg * GROUP + jj
-            for m in range(count):
-                tile = tops[m]
-                first = jnp.broadcast_to(tile[:, j : j + 1], shape)
-                second = jnp.broadcast_to(tile[:, j + 1 : j + 2], shape)
-                p00, p01, p11 = first[jj : jj + 1], second[jj : jj + 1], second[jj + 1 : jj + 2]
-                r0, r1 = tile[jj : jj + 1], tile[jj + 1 : jj + 2]
-                inverse = 1.0 / (p00 * p11 - p01 * p01)
-                cross = p01 * inverse
-                t0 = (p11 * inverse) * r0 - cross * r1
-                t1 = (p00 * inverse) * r1 - cross * r0
-                lower = tile - first * t0 - second * t1
-                tops[m] = jnp.where(
-                    subs > jj + 1, lower, jnp.where(subs == jj + 1, tile - (p01 / p00) * r0, tile)
-                )
-                if jg < B // GROUP - 1:
-                    rest = diag[m, jg * GROUP + GROUP :, :]
-                    diag[m, jg * GROUP + GROUP :, :] = (
-                        rest - rest[:, j : j + 1] * t0 - rest[:, j + 1 : j + 2] * t1
-                    )
-        for m in range(count):
-            diag[m, top, :] = tops[m]
-
-
-def orthonormal(count, work, diag):
-    row = lax.broadcasted_iota(jnp.int32, (B, 2 * B), 0)
-    lane = lax.broadcasted_iota(jnp.int32, (B, 2 * B), 1)
-    def load(k):
+INS, OUTS = 7, 5
+
+
+def eliminate_group(diag, jg):
+    count = diag.shape[0]
+    shape = (count, GROUP, 2 * B)
+    subs = lax.broadcasted_iota(jnp.int32, shape, 1)
+    top = slice(jg * GROUP, jg * GROUP + GROUP)
+    tile = diag[:, top, :]
+    for jj in range(0, GROUP, 2):
+        j = jg * GROUP + jj
+        first = jnp.broadcast_to(tile[:, :, j : j + 1], shape)
+        second = jnp.broadcast_to(tile[:, :, j + 1 : j + 2], shape)
+        p00, p01, p11 = first[:, jj : jj + 1], second[:, jj : jj + 1], second[:, jj + 1 : jj + 2]
+        r0, r1 = tile[:, jj : jj + 1], tile[:, jj + 1 : jj + 2]
+        inverse = 1.0 / (p00 * p11 - p01 * p01)
+        cross = p01 * inverse
+        t0 = (p11 * inverse) * r0 - cross * r1
+        t1 = (p00 * inverse) * r1 - cross * r0
+        lower = tile - first * t0 - second * t1
+        tile = jnp.where(subs > jj + 1, lower, jnp.where(subs == jj + 1, tile - (p01 / p00) * r0, tile))
+        if jg < B // GROUP - 1:
+            rest = diag[:, jg * GROUP + GROUP :, :]
+            diag[:, jg * GROUP + GROUP :, :] = (
+                rest - rest[:, :, j : j + 1] * t0 - rest[:, :, j + 1 : j + 2] * t1
+            )
+    diag[:, top, :] = tile
+
+
+class Update:
+    def __init__(self, slots, begin, shift, sums, ins, outs, inbuf, outbuf, qbuf, work, diag, in_sem, out_sem, q_sem):
+        self.slots, self.begin, self.shift = slots, begin, shift
+        self.sums, self.ins, self.outs = sums, ins, outs
+        self.inbuf, self.outbuf, self.qbuf, self.work, self.diag = inbuf, outbuf, qbuf, work, diag
+        self.in_sem, self.out_sem, self.q_sem = in_sem, out_sem, q_sem
+
+    def fetch(self):
+        for s in range(self.slots):
+            for n in range(INS):
+                pltpu.make_async_copy(self.ins[n].at[self.begin + s], self.inbuf.at[s, n], self.in_sem.at[s]).start()
+
+    def refine(self, s):
+        pltpu.make_async_copy(self.inbuf.at[s], self.inbuf.at[s], self.in_sem.at[s]).wait()
+        place = s % 2
+        if s >= 2:
+            pltpu.make_async_copy(self.outbuf.at[place], self.outbuf.at[place], self.out_sem.at[place]).wait()
+        w, m1, m2, ls, rs, lb, rb = (self.inbuf.at[s, n] for n in range(INS))
+        wn, m1n, m2n, lsn, rsn = (self.outbuf.at[place, n] for n in range(OUTS))
+        e = split(self.sums[s * T : (s + 1) * T, :])
+        ql = split(lb[...])
+        qr = split(rb[...])
+        left = BETA_TWO * ls[...] + (1.0 - BETA_TWO) * mm3(e, e, NT)
+        right = BETA_TWO * rs[...] + (1.0 - BETA_TWO) * mm3(e, e, TN)
+        lsn[...] = left
+        rsn[...] = right
+        turned = mm3(split(mm3(ql, e, TN)), qr, NN)
+        first = BETA_ONE * m1[...] + (1.0 - BETA_ONE) * turned
+        second = BETA_TWO * m2[...] + (1.0 - BETA_TWO) * turned * turned
+        m1n[...] = first
+        m2n[...] = second
+        direction = mm3(split(mm3(ql, split(adam_step(first, second)), NN)), qr, NT)
+        old = w[...]
+        wn[...] = old - RATE_MATRIX * (direction + DECAY * old)
+        for n in range(OUTS):
+            pltpu.make_async_copy(self.outbuf.at[place, n], self.outs[n].at[self.shift + s], self.out_sem.at[place]).start()
+        for side, (basis, stat) in enumerate(((ql, left), (qr, right))):
+            y = mm3(basis, split(stat), TN)
+            y = y * lax.rsqrt(jnp.sum(y * y, axis=1, keepdims=True))
+            self.work[2 * s + side, :, T:] = y
+            y = split(y)
+            self.work[2 * s + side, :, :T] = mm3(y, y, NT)
+
+    def load(self, k):
         low = k * B
         edge = low // (2 * B) * 2 * B
-        for m in range(count):
-            block = work[m, low : low + B, edge : edge + 2 * B]
+        row = lax.broadcasted_iota(jnp.int32, (B, 2 * B), 0)
+        lane = lax.broadcasted_iota(jnp.int32, (B, 2 * B), 1)
+        for m in range(2 * self.slots):
+            block = self.work[m, low : low + B, edge : edge + 2 * B]
             if low % (2 * B):
                 block = pltpu.roll(block, B, 1)
-            diag[m] = jnp.where(lane < B, block, jnp.where(lane == row + B, 1.0, 0.0))
-
-    def products(k):
+            self.diag[m] = jnp.where(lane < B, block, jnp.where(lane == row + B, 1.0, 0.0))
+
+    def products(self, k, begin, end):
         low = k * B
         edge = low // (2 * B) * 2 * B
-
-        def apply(step, _):
-            for n in range(ABREAST):
-                m = step * ABREAST + n
-                d = diag[m]
-                pivots = jnp.sum(jnp.where(lane == row, d, 0.0), axis=1, keepdims=True)
-                high, rest = split(d[:, B:] * lax.rsqrt(pivots))
-                inverse = jnp.concatenate([high, rest, high], 1)
-                high, rest = split(work[m, low : low + B, edge:])
-                new = dot(inverse, jnp.concatenate([high, high, rest], 0), NN)
-                work[m, low : low + B, edge:] = new
-                if low + B < T:
-                    high, rest = split(new)
-                    after = low + B - edge
-                    begin = (low + B) // (2 * B) * 2 * B
-                    left = jnp.concatenate([high, rest, high], 0)[:, after : T - edge]
-                    right = jnp.concatenate([high, high, rest], 0)[:, begin - edge :]
-                    work[m, low + B :, begin:] = work[m, low + B :, begin:] - dot(left, right, TN)
+        row = lax.broadcasted_iota(jnp.int32, (B, 2 * B), 0)
+        lane = lax.broadcasted_iota(jnp.int32, (B, 2 * B), 1)
+        work = self.work
+
+        def one(m):
+            d = self.diag[m]
+            pivots = jnp.sum(jnp.where(lane == row, d, 0.0), axis=1, keepdims=True)
+            high, rest = split(d[:, B:] * lax.rsqrt(pivots))
+            inverse = jnp.concatenate([high, rest, high], 1)
+            high, rest = split(work[m, low : low + B, edge:])
+            new = dot(inverse, jnp.concatenate([high, high, rest], 0), NN)
+            work[m, low : low + B, edge:] = new
+            if low + B < T:
+                high, rest = split(new)
+                after = low + B - edge
+                start = (low + B) // (2 * B) * 2 * B
+                left = jnp.concatenate([high, rest, high], 0)[:, after : T - edge]
+                right = jnp.concatenate([high, high, rest], 0)[:, start - edge :]
+                work[m, low + B :, start:] = work[m, low + B :, start:] - dot(left, right, TN)
+
+        def pair(i, _):
+            one(begin + 2 * i)
+            one(begin + 2 * i + 1)
             return 0
 
-        lax.fori_loop(0, count // ABREAST, apply, 0)
-
-    def block(k, _):
-        for which in range(T // B):
-            pl.when(k == which)(functools.partial(load, which))
-        eliminate(count, diag)
-        for which in range(T // B):
-            pl.when(k == which)(functools.partial(products, which))
-        return 0
-
-    lax.fori_loop(0, T // B, block, 0)
-
-
-def optimizer_body(slots, g_ref, vg_ref, w_ref, m1_ref, m2_ref, ls_ref, rs_ref, lb_ref, rb_ref, vw_ref, v1_ref, v2_ref,
-                   wn_ref, m1n_ref, m2n_ref, lsn_ref, rsn_ref, lbn_ref, rbn_ref, vwn_ref, v1n_ref, v2n_ref, work, diag):
-    i = pl.program_id(0)
-
-    @pl.when(i == 0)
-    def _():
-        for k in range(vw_ref.shape[1] // T):
-            cols = slice(k * T, (k + 1) * T)
-            g = vg_ref[k : k + 1, :]
-            first = BETA_ONE * v1_ref[:, cols] + (1.0 - BETA_ONE) * g
-            second = BETA_TWO * v2_ref[:, cols] + (1.0 - BETA_TWO) * g * g
-            v1n_ref[:, cols] = first
-            v2n_ref[:, cols] = second
-            vwn_ref[:, cols] = vw_ref[:, cols] - RATE_VECTOR * adam_step(first, second)
-
-    refine(i, slots, g_ref, w_ref, m1_ref, m2_ref, ls_ref, rs_ref, lb_ref, rb_ref,
-           wn_ref, m1n_ref, m2n_ref, lsn_ref, rsn_ref, work)
-
-    @pl.when(i == slots - 1)
-    def _():
-        orthonormal(work.shape[0], work, diag)
-
-        def finish(m, _):
-            lbn_ref[m] = work[m, :, T:].T
-            rbn_ref[m] = work[slots + m, :, T:].T
-            return 0
-
-        lax.fori_loop(0, slots, finish, 0)
-
-
-def optimizer(g, w, m1, m2, ls, rs, lb, rb, vw, v1, v2):
-    slots = w.shape[0]
-    count = -(-2 * slots // ABREAST) * ABREAST
-    one = pl.BlockSpec((1, T, T), lambda i: (i, 0, 0))
-    every = pl.BlockSpec((slots, T, T), lambda i: (0, 0, 0))
-    line = pl.BlockSpec(vw.shape, lambda i: (0, 0))
+        lax.fori_loop(0, (end - begin) // 2, pair, 0)
+
+    def finish(self, s):
+        for side in range(2):
+            if s:
+                pltpu.make_async_copy(self.qbuf.at[side], self.qbuf.at[side], self.q_sem.at[side]).wait()
+            self.qbuf[side] = self.work[2 * s + side, :, T:].T
+            pltpu.make_async_copy(self.qbuf.at[side], self.outs[OUTS + side].at[self.shift + s], self.q_sem.at[side]).start()
+
+    def close(self):
+        for side in range(2):
+            pltpu.make_async_copy(self.qbuf.at[side], self.qbuf.at[side], self.q_sem.at[side]).wait()
+        for place in range(min(2, self.slots)):
+            pltpu.make_async_copy(self.outbuf.at[place], self.outbuf.at[place], self.out_sem.at[place]).wait()
+
+    def steps(self):
+        result = [functools.partial(self.refine, s) for s in range(self.slots)]
+        for k in range(T // B):
+            result.append(functools.partial(self.load, k))
+            result += [functools.partial(eliminate_group, self.diag, jg) for jg in range(B // GROUP)]
+            middle = self.slots // 2 * 2
+            result += [functools.partial(self.products, k, a, b) for a, b in ((0, middle), (middle, 2 * self.slots)) if a < b]
+        result += [functools.partial(self.finish, s) for s in range(self.slots)]
+        result.append(self.close)
+        return result
+
+
+def update_scratch(slots):
     f32 = jnp.float32
+    dma = pltpu.SemaphoreType.DMA
+    return [
+        pltpu.VMEM((slots, INS, T, T), f32),
+        pltpu.VMEM((2, OUTS, T, T), f32),
+        pltpu.VMEM((2, T, T), f32),
+        pltpu.VMEM((2 * slots, T, 2 * T), f32),
+        pltpu.VMEM((2 * slots, B, 2 * B), f32),
+        dma((slots,)),
+        dma((2,)),
+        dma((2,)),
+    ]
+
+
+def rest_body(total, done, sums_ref, v_refs, ins, befores, outs, v_outs, scratch, passing, passing_sem):
+    update = Update(total - done, done, done, sums_ref, ins, outs, *scratch)
+    update.fetch()
+    arrivals = [
+        pltpu.make_async_copy(before, passing.at[n], passing_sem.at[0, n]) for n, before in enumerate(befores)
+    ]
+    departures = [
+        pltpu.make_async_copy(passing.at[n], outs[n].at[pl.ds(0, done)], passing_sem.at[1, n])
+        for n in range(len(befores))
+    ]
+    for copy in arrivals:
+        copy.start()
+    vw_ref, v1_ref, v2_ref = v_refs
+    vwn_ref, v1n_ref, v2n_ref = v_outs
+    for k in range(vw_ref.shape[1] // T):
+        cols = slice(k * T, (k + 1) * T)
+        row = (total - done) * T + k
+        g = sums_ref[row : row + 1, :]
+        first = BETA_ONE * v1_ref[:, cols] + (1.0 - BETA_ONE) * g
+        second = BETA_TWO * v2_ref[:, cols] + (1.0 - BETA_TWO) * g * g
+        v1n_ref[:, cols] = first
+        v2n_ref[:, cols] = second
+        vwn_ref[:, cols] = vw_ref[:, cols] - RATE_VECTOR * adam_step(first, second)
+    for number, step in enumerate(update.steps()):
+        step()
+        if number == total - done - 1:
+            for arrival, departure in zip(arrivals, departures):
+                arrival.wait()
+                departure.start()
+    for copy in departures:
+        copy.wait()
+
+
+def optimizer(sums, states, vectors, befores=()):
+    total = states[0].shape[0]
+    done = befores[0].shape[0] if befores else 0
+    hbm = pl.BlockSpec(memory_space=pl.ANY)
+    vmem = pl.BlockSpec(memory_space=pltpu.VMEM)
+    f32 = jnp.float32
+    count = len(befores)
+
+    def body(*refs):
+        sums_ref, v_refs, refs = refs[0], refs[1:4], refs[4:]
+        ins, befores, refs = refs[:INS], refs[INS : INS + count], refs[INS + count :]
+        outs, v_outs, refs = refs[:INS], refs[INS : INS + 3], refs[INS + 3 :]
+        rest_body(total, done, sums_ref, v_refs, ins, befores, outs, v_outs, refs[:-2], *refs[-2:])
+
     return pl.pallas_call(
-        functools.partial(optimizer_body, slots),
-        grid=(slots,),
-        in_specs=[
-            pl.BlockSpec((T, T), lambda i: (i, 0)),
-            pl.BlockSpec((EXTRA, T), lambda i: (slots * T // EXTRA, 0)),
-        ]
-        + [one] * 7
-        + [line] * 3,
-        out_specs=[one] * 5 + [every] * 2 + [line] * 3,
-        out_shape=[jax.ShapeDtypeStruct(w.shape, f32)] * 7 + [jax.ShapeDtypeStruct(vw.shape, f32)] * 3,
-        scratch_shapes=[
-            pltpu.VMEM((count, T, 2 * T), f32),
-            pltpu.VMEM((count, B, 2 * B), f32),
-        ],
+        body,
+        in_specs=[vmem] * 4 + [hbm] * (INS + count),
+        out_specs=[hbm] * INS + [vmem] * 3,
+        out_shape=[jax.ShapeDtypeStruct(v.shape, f32) for v in (*states, *vectors)],
+        scratch_shapes=update_scratch(total - done)
+        + [pltpu.VMEM((INS, max(done, 1), T, T), f32), pltpu.SemaphoreType.DMA((2, INS))],
         compiler_params=pltpu.CompilerParams(vmem_limit_bytes=60 << 20),
         name="optimizer",
-    )(g, g, w, m1, m2, ls, rs, lb, rb, vw, v1, v2)
+    )(sums, *vectors, *states, *befores)
 
 
 ORDERS = ("xzy", "yzx", "zxy", "zyx")
@@ -716,7 +764,7 @@
             fixed[key] = max(times[key], time_of(parent) + 0.01)
         return fixed[key]
 
-    return sorted(times, key=lambda k: (time_of(k), k))
+    return sorted((time_of(k), k) for k in times)
 
 
 class Place:
@@ -877,7 +925,7 @@
     hbm = pl.BlockSpec(memory_space=pl.ANY)
     dma = pltpu.SemaphoreType.DMA
     return pl.pallas_call(
-        functools.partial(gather_body, depth, parts, plan_of(depth)),
+        functools.partial(gather_body, depth, parts, [key for _, key in plan_of(depth)]),
         in_specs=[hbm, pl.BlockSpec(memory_space=pltpu.VMEM)],
         out_specs=hbm,
         out_shape=jax.ShapeDtypeStruct((8 * depth, rows, T), jnp.bfloat16),
@@ -916,22 +964,54 @@
         piece(whole * 128, size % 128)
 
 
-def reduce_body(depth, parts, plan, grads_ref, out_ref, acc, twin, flat0, flat1, line, *sems):
-    load_sem, twin_send, twin_recv, flat0_send, flat0_recv, flat1_send, flat1_recv, line_send, line_recv = sems
+LOADS = 8
+
+
+def wave_rows(slots, early):
+    result = []
+    for begin, count, extra in ((0, early, 0), (early * T, slots - early, EXTRA)):
+        size = count * T // 4
+        sizes = [size, size, size, size + extra]
+        result += [(begin + sum(sizes[:i]), sizes[i]) for i in range(4)]
+    return result
+
+
+def wave_keys(depth, slots, early):
+    timed = plan_of(depth)
+    end = timed[-1][0]
+    share = early / slots
+    result = []
+    for wave in range(2):
+        for when, (part, *key) in timed + [(0.0, (part, 0, 0, 0)) for part in range(4)]:
+            spent = end - when
+            at = spent * share if wave == 0 else end * (share - 0.06) + spent * (1 - share)
+            result.append((at, wave, -len(result), 4 * wave + part, tuple(key)))
+    return [(part, key) for _, _, _, part, key in sorted(result)]
+
+
+def reduce_body(depth, slots, early, parts, keys, grads_ref, *refs):
+    ins, refs = refs[:INS], refs[INS:]
+    late_ref, refs = refs[0], refs[1:]
+    outs, refs = refs[:INS], refs[INS:]
+    (own, twin, sums, flat0_a, flat0_b, flat1_a, flat1_b, line_a, line_b,
+     load_sem, twin_send, twin_recv, flat0_send, flat0_recv, flat1_send, flat1_recv, line_send, line_recv) = refs[:18]
+    update = Update(early, 0, 0, sums, ins, outs, *refs[18:])
     here = Place(depth)
-    keys = [(part, tuple(key)) for part, *key in reversed(plan)] + [(part, (0, 0, 0)) for part in range(4)]
-    loads = []
-    for part, key in keys:
-        if key not in loads:
-            loads.append(key)
-    for key in loads:
+
+    def load(number):
+        part, key = keys[number]
         cell = here.at(*key)
+        start, size = parts[part]
+        place = number % LOADS
         guarded(
             [here.inside(key[0])],
             pltpu.make_async_copy(
-                grads_ref.at[here.block(cell)], acc.at[here.spot(cell)], load_sem.at[here.spot(cell)]
+                grads_ref.at[here.block(cell), pl.ds(start, size)], own.at[place, pl.ds(0, size)], load_sem.at[place]
             ).start,
         )
+
+    for number in range(LOADS):
+        load(number)
     here.meet()
     other = here.device(here.at(), True)
     for part, key in keys:
@@ -945,144 +1025,166 @@
                 twin_recv.at[part, spot], other,
             ).start,
         )
+    update.fetch()
     for end, shift in ((0, 1), (depth - 1, 0)):
 
         def clear():
-            for part in range(4):
-                columns = 2 if ORDERS[part][1] == "z" else 1
-                for column in range(columns):
+            for line in (line_a, line_b):
+                for row in range(6):
                     for target in range(depth):
-                        place = line.at[part, column, target + shift]
+                        place = line.at[row * (depth + 1) + target + shift]
                         place[...] = jnp.zeros(place.shape, place.dtype)
 
         pl.when(here.z == end)(clear)
     waits = []
-    loaded = set()
-    for part, key in keys:
+
+    def task(number):
+        part, key = keys[number]
+        wave, local = part // 4, part % 4
+        flat0, flat1, line = (flat0_a, flat1_a, line_a) if wave == 0 else (flat0_b, flat1_b, line_b)
         start, size = parts[part]
         rows = pl.ds(start, size)
         short = pl.ds(0, size)
-        first, second, third = reversed(ORDERS[part])
-        away = {"z": key[0], "x": key[1], "y": key[2]}
+        order = ORDERS[local]
         cell = here.at(*key)
         spot = here.spot(cell)
         present = here.inside(key[0])
-        step = last_step(ORDERS[part], key)
-        index0 = cell[0] * 2 + (cell[1] if first == "y" else cell[2])
-
-        def task(part=part, key=key, start=start, size=size, rows=rows, short=short, step=step, cell=cell,
-                 spot=spot, first=first, second=second, third=third, away=away, index0=index0):
-            if key not in loaded:
-                drain(acc.at[spot], load_sem.at[spot])
-            drain(twin.at[spot, rows], twin_recv.at[part, spot])
-            mine = acc.at[spot, rows]
-            sources = [mine, twin.at[spot, rows]]
-            order = ORDERS[part]
-            column = 0
-            if order[1] == "z":
-                column = cell[1] if order[0] == "x" else cell[2]
+        step = last_step(order, key)
+        middle = order[1] == "z"
+        cross = order[2]
+        index0 = local * 2 * depth + cell[0] * 2 + (cell[1] if cross == "y" else cell[2])
+        if middle:
+            row = local * 2 + (cell[1] if order[0] == "x" else cell[2])
+            index1 = local
+        else:
+            row = local + 2
+            index1 = 2 + (local - 2) * depth + cell[0]
+        line0 = row * (depth + 1) + cell[0]
+        sent = row * depth + cell[0]
+        base0, base1, base_line, base_sent = (wave * n for n in (8 * depth, 2 + 2 * depth, 6 * (depth + 1), 6 * depth))
+
+        def run():
+            mine = own.at[number % LOADS, short]
+            target = twin.at[spot, rows]
+            drain(mine, load_sem.at[number % LOADS])
+            drain(target, twin_recv.at[part, spot])
+            sources = [mine, target]
             for i in (2, 1, 0):
                 if i <= step - 1 or (i == step and order[i] != "z"):
                     break
-                if i == 2 and order[i] != "z":
-                    drain(flat0.at[part, index0, short], flat0_recv.at[part, index0])
-                    sources.append(flat0.at[part, index0, short])
-                elif order[i] != "z":
-                    which = cell[0] if i == 1 else 0
-                    drain(flat1.at[part, which, short], flat1_recv.at[part, which])
-                    sources.append(flat1.at[part, which, short])
-                else:
+                if order[i] == "z":
                     ways = (1, 0)
                     if i == step:
                         ways = (1,) if key[0] > 0 else (0,)
                     for way in ways:
-                        place = line.at[part, column, cell[0] + way, short]
-
-                        def arrive(place=place, way=way):
-                            drain(place, line_recv.at[part, column, cell[0] + way])
-
+                        place = line.at[line0 + way, short]
+                        arrive = functools.partial(drain, place, line_recv.at[base_line + line0 + way])
                         pl.when(here.z > 0 if way else here.z < depth - 1)(arrive)
                         sources.append(place)
                     if i == step:
                         break
+                elif i == 2:
+                    drain(flat0.at[index0, short], flat0_recv.at[base0 + index0])
+                    sources.append(flat0.at[index0, short])
+                else:
+                    drain(flat1.at[index1, short], flat1_recv.at[base1 + index1])
+                    sources.append(flat1.at[index1, short])
             if step < 0:
-                add_rows(size, out_ref, start, sources)
+                add_rows(size, sums, start, sources)
                 return
-            add_rows(size, acc.at[spot], start, sources)
+            add_rows(size, twin.at[spot], start, sources)
             dim = order[step]
             if dim == "z":
                 way = 1 if key[0] > 0 else 0
                 remote(
-                    mine, line.at[part, column, cell[0] + way, short], line_send.at[part, column, cell[0]],
-                    line_recv.at[part, column, cell[0] + way], here.device(here.at(dz=1 if way else -1)),
+                    target, line.at[line0 + way, short], line_send.at[base_sent + sent],
+                    line_recv.at[base_line + line0 + way], here.device(here.at(dz=1 if way else -1)),
                 ).start()
                 return
-            target = here.device(here.at(dx=1) if dim == "x" else here.at(dy=1))
+            device = here.device(here.at(dx=1) if dim == "x" else here.at(dy=1))
             if step == 2:
                 remote(
-                    mine, flat0.at[part, index0, short], flat0_send.at[part], flat0_recv.at[part, index0], target
+                    target, flat0.at[index0, short], flat0_send.at[part], flat0_recv.at[base0 + index0], device
                 ).start()
             else:
-                which = cell[0] if step == 1 else 0
                 remote(
-                    mine, flat1.at[part, which, short], flat1_send.at[part], flat1_recv.at[part, which], target
+                    target, flat1.at[index1, short], flat1_send.at[part], flat1_recv.at[base1 + index1], device
                 ).start()
 
-        guarded([present], task)
-        loaded.add(key)
-        if step >= 0 and ORDERS[part][step] == "z":
-            column = 0
-            if ORDERS[part][1] == "z":
-                column = cell[1] if ORDERS[part][0] == "x" else cell[2]
+        guarded([present], run)
+        if number + LOADS < len(keys):
+            load(number + LOADS)
+        if step >= 0 and order[step] == "z":
             waits.append(
-                ([present], functools.partial(drain, acc.at[spot, rows], line_send.at[part, column, cell[0]]))
+                ([present], functools.partial(drain, twin.at[spot, rows], line_send.at[base_sent + sent]))
             )
+
+    ready = max(n for n, (part, key) in enumerate(keys) if part < 4)
+    steps = update.steps()
+    taken = 0
+    for number in range(len(keys)):
+        task(number)
+        if number >= ready:
+            due = len(steps) * (number - ready + 1) // (len(keys) - ready)
+            for step in steps[taken:due]:
+                step()
+            taken = due
+    late_ref[...] = sums[early * T :, :]
     for conditions, action in waits:
         guarded(conditions, action)
-    for part in range(4):
+    for part in range(8):
         rows = pl.ds(*parts[part])
-        order = ORDERS[part]
+        order = ORDERS[part % 4]
         sent = 1
         for i, dim in enumerate(order):
             if dim != "z":
                 sem = flat0_send if i == 2 else flat1_send
-                drain(acc.at[pl.ds(0, sent), rows], sem.at[part])
+                drain(twin.at[pl.ds(0, sent), rows], sem.at[part])
             sent *= depth if dim == "z" else 2
-    drain(acc, twin_send)
-
-
-def reduce_blocks(depth, slots, grads):
-    parts = part_rows(slots)
+    drain(twin, twin_send)
+
+
+def reduce_and_start(depth, grads, states):
+    slots = states[0].shape[0]
+    early = slots * 5 // 8
+    parts = wave_rows(slots, early)
     rows = grads.shape[1]
-    longest = max(size for _, size in parts)
+    long_a, long_b = parts[3][1], parts[7][1]
     dma = pltpu.SemaphoreType.DMA
-    bf = jnp.bfloat16
+    bf, f32 = jnp.bfloat16, jnp.float32
+    hbm = pl.BlockSpec(memory_space=pl.ANY)
     return pl.pallas_call(
-        functools.partial(reduce_body, depth, parts, plan_of(depth)),
-        in_specs=[pl.BlockSpec(memory_space=pl.ANY)],
-        out_specs=pl.BlockSpec(memory_space=pltpu.VMEM),
-        out_shape=jax.ShapeDtypeStruct((rows, T), jnp.float32),
+        functools.partial(reduce_body, depth, slots, early, parts, wave_keys(depth, slots, early)),
+        in_specs=[hbm] * (1 + INS),
+        out_specs=[pl.BlockSpec(memory_space=pltpu.VMEM)] + [hbm] * INS,
+        out_shape=[jax.ShapeDtypeStruct((rows - early * T, T), f32)]
+        + [jax.ShapeDtypeStruct((early, T, T), f32)] * INS,
         scratch_shapes=[
+            pltpu.VMEM((LOADS, max(long_a, long_b), T), bf),
             pltpu.VMEM((4 * depth, rows, T), bf),
-            pltpu.VMEM((4 * depth, rows, T), bf),
-            pltpu.VMEM((4, 2 * depth, longest, T), bf),
-            pltpu.VMEM((4, depth, longest, T), bf),
-            pltpu.VMEM((4, 2, depth + 1, longest, T), bf),
-            dma((4 * depth,)),
+            pltpu.VMEM((rows, T), f32),
+            pltpu.VMEM((8 * depth, long_a, T), bf),
+            pltpu.VMEM((8 * depth, long_b, T), bf),
+            pltpu.VMEM((2 + 2 * depth, long_a, T), bf),
+            pltpu.VMEM((2 + 2 * depth, long_b, T), bf),
+            pltpu.VMEM((6 * (depth + 1), long_a, T), bf),
+            pltpu.VMEM((6 * (depth + 1), long_b, T), bf),
+            dma((LOADS,)),
             dma,
-            dma((4, 4 * depth)),
-            dma((4,)),
-            dma((4, 2 * depth)),
-            dma((4,)),
-            dma((4, depth)),
-            dma((4, 2, depth)),
-            dma((4, 2, depth + 1)),
-        ],
+            dma((8, 4 * depth)),
+            dma((8,)),
+            dma((16 * depth,)),
+            dma((8,)),
+            dma((4 + 4 * depth,)),
+            dma((12 * depth,)),
+            dma((12 * (depth + 1),)),
+        ]
+        + update_scratch(early),
         compiler_params=pltpu.CompilerParams(
             collective_id=1, has_side_effects=True, vmem_limit_bytes=63 << 20
         ),
-        name="reduce_blocks",
-    )(grads)
+        name="reduce_and_start",
+    )(grads, *states)
 
 
 def grid_depth():
@@ -1099,13 +1201,6 @@
     own = jnp.concatenate([tiles.reshape(-1, T), vec.reshape(-1, T)], 0)
     own = jnp.pad(own, ((0, EXTRA - vec.size // T), (0, 0))).astype(jnp.bfloat16)
     return lax.all_gather(own, ("tower", "batch"), axis=0)
-
-
-def own_sums(slots, grads):
-    depth = grid_depth()
-    if depth is not None:
-        return reduce_blocks(depth, slots, grads)
-    return lax.psum_scatter(grads, ("tower", "batch"), scatter_dimension=0).astype(jnp.float32)
 
 
 def per_device(
@@ -1133,20 +1228,15 @@
     concat, text_grad, grads = tower(
         True, slots, tile_slot, caption_lengths, text_rows, concat_cot, copies, (projected, grads)
     )
-    states = optimizer(
-        own_sums(slots, grads),
-        tile_weight,
-        tile_first,
-        tile_second,
-        left_stat,
-        right_stat,
-        left_basis,
-        right_basis,
-        vec_weight,
-        vec_first,
-        vec_second,
-    )
-    return (concat, image_grad, text_grad, *states)
+    states = (tile_weight, tile_first, tile_second, left_stat, right_stat, left_basis, right_basis)
+    depth = grid_depth()
+    if depth is not None:
+        sums, *befores = reduce_and_start(depth, grads, states)
+    else:
+        sums = lax.psum_scatter(grads, ("tower", "batch"), scatter_dimension=0).astype(jnp.float32)
+        befores = ()
+    news = optimizer(sums, states, (vec_weight, vec_first, vec_second), befores)
+    return (concat, image_grad, text_grad, *news)
 
 
 def solution(mesh):

time: 441 us -> 418 us (0.948)
  Pallas kernels: 438 us -> 414 us
    pallas_call x3, Pallas kernels: 335 us -> 311 us  [the longest x1 146 us: reduce_and_start(): pl.pallas_call(functools.partial(reduce_body, depth, slots, early, parts,...]
where the time goes in v2:
time: 418 us; the launch traced here: 415 us
  Pallas kernels  414 us (99%)
    pallas_call x1, Pallas kernels, reduce_and_start(): pl.pallas_call(functools.partial(reduce_body, depth, slots, early, parts,...  146 us
    pallas_call x1, Pallas kernels, gather(): pl.pallas_call(functools.partial(gather_body, depth, parts, [key for _, k...  127 us
    pallas_call x2, Pallas kernels, tower(): pl.pallas_call(functools.partial(tower_body, is_text, rows, slots), in_sp...  103 us
    pallas_call x1, Pallas kernels, optimizer(): pl.pallas_call(body, in_specs=[vmem] * 4 + [hbm] * (INS + count), out_spe...  37.6 us

profile of v2, /device:TPU:18, one launch (start us, length us, event | category | flops | bytes accessed | tf_op | source)
XLA Modules:
  0.0 414.5 jit_solution(12993663114763985286)
XLA Ops:
  0.6 127.0 %gather.1.copies = bf16[32,2064,256]{2,1,0:T(8,128)(2,1)} custom-call(f32[8,256,256]{2,1,0:T(8,128)} %refs_4_.3, f32[1,768]{1,0:T(1,128)} %refs_1_.3), custom_call_target="tpu_custom_call" | custom-call | tf_op jit(solution)/shard_map/gather/pallas_call | solution.py:927
  127.7 39.5 %image_tower.1 = (bf16[1,197,768]{2,1,0:T(8,128)(2,1)}, bf16[1,197,768]{2,1,0:T(8,128)(2,1)}, bf16[32,2064,256]{2,1,0:T(8,128)(2,1)}) custom-call(s32[234]{0:T(256)} %slot_ref.3, s32[32]{0:T(128)} %length_ref.3, bf16[1,197,768]{2,1,0:T(8,128)(2,1)} %x_ref.2, bf16[1,711,768]{2,1,0:T(8,128)(2,1)} %cot_ref.3, bf16[32,2064,256]{2,1,0:T(8,128)(2,1)} %gather.1.copies), custom_call_target="tpu_custom_call" | custom-call | tf_op jit(solution)/shard_map/image_tower/pallas_call | solution.py:444
  167.1 63.5 %text_tower.1 = (bf16[1,711,768]{2,1,0:T(8,128)(2,1)}, bf16[1,512,768]{2,1,0:T(8,128)(2,1)}, bf16[32,2064,256]{2,1,0:T(8,128)(2,1)}) custom-call(s32[234]{0:T(256)} %slot_ref.3, s32[32]{0:T(128)} %length_ref.3, bf16[1,512,768]{2,1,0:T(8,128)(2,1)} %x_ref.3, bf16[1,711,768]{2,1,0:T(8,128)(2,1)} %cot_ref.3, ...), custom_call_target="tpu_custom_call", output_to_operand_aliasing={{2}: (6, {})} | custom-call | tf_op jit(solution)/shard_map/text_tower/pallas_call | solution.py:444
  230.6 146.0 %reduce_and_start.1 = (f32[784,256]{1,0:T(8,128)}, f32[5,256,256]{2,1,0:T(8,128)}, f32[5,256,256]{2,1,0:T(8,128)}, f32[5,256,256]{2,1,0:T(8,128)}, f32[5,256,256...) custom-call(bf16[32,2064,256]{2,1,0:T(8,128)(2,1)} %get-tuple-element.42.grads_ref, ...), custom_call_target="tpu_custom_call" | custom-call | tf_op jit(solution)/shard_map/reduce_and_start/pallas_call | solution.py:1156
  376.7 37.6 %optimizer.1 = (f32[8,256,256]{2,1,0:T(8,128)}, f32[8,256,256]{2,1,0:T(8,128)}, f32[8,256,256]{2,1,0:T(8,128)}, f32[8,256,256]{2,1,0:T(8,128)}, f32[8,256,256]{2...) custom-call(f32[784,256]{1,0:T(8,128)} %get-tuple-element.43.refs_0_, ...), custom_call_target="tpu_custom_call" | custom-call | tf_op jit(solution)/shard_map/optimizer/pallas_call | solution.py:680

commit v3 on v2

--- a/solution.py
+++ b/solution.py
@@ -223,7 +223,7 @@
         o[:, pair_cols(p, 0)] = rounded(jnp.where(lane < HEAD_DIM, outs[0], outs[1]))
         return 0
 
-    lax.fori_loop(0, HEADS // 2, attend, 0)
+    lax.fori_loop(0, HEADS // 2, attend, 0, unroll=True)
     ot[...] = o[...].T
     drain(wo, wsem.at[1])
     a[...] = mm(o[...], wo[...])
@@ -246,7 +246,7 @@
         ht[cols, :] = hidden.T
         return 0
 
-    lax.fori_loop(0, FF // WIDE, up, 0)
+    lax.fori_loop(0, FF // WIDE, up, 0, unroll=2)
     drain(wd, wsem.at[3])
     y[...] = mm(h[...], wd[...])
     for c in chunks:
@@ -319,7 +319,7 @@
         put(place, tiles)
         return 0
 
-    lax.fori_loop(0, FF // WIDE, down, 0)
+    lax.fori_loop(0, FF // WIDE, down, 0, unroll=True)
     for i in range(FF // D):
         vec_grad(7 + i, bias_up[:, i * D : (i + 1) * D])
     da[...] = mm(du[...], wu[...], NT)
@@ -379,7 +379,7 @@
         dqkv[:, pair_cols(p, 2 * D)] = rounded(jnp.concatenate(dvs, 0).T)
         return 0
 
-    lax.fori_loop(0, HEADS // 2, attend_back, 0)
+    lax.fori_loop(0, HEADS // 2, attend_back, 0, unroll=True)
     for m, number in ((0, 2), (2, 3)):
         vec_grad(number, jnp.sum(dqkv[:, m * D : (m + 1) * D].astype(jnp.float32), 0, keepdims=True))
     for m in range(3):
@@ -588,7 +588,7 @@
             one(begin + 2 * i + 1)
             return 0
 
-        lax.fori_loop(0, (end - begin) // 2, pair, 0)
+        lax.fori_loop(0, (end - begin) // 2, pair, 0, unroll=True)
 
     def finish(self, s):
         for side in range(2):

time: 418 us -> 404 us (0.967)
  Pallas kernels: 414 us -> 397 us
    pallas_call x2, Pallas kernels: 103 us -> 92.6 us  [tower(): pl.pallas_call(functools.partial(tower_body, is_text, rows, slots), in_sp...]
    pallas_call x1, Pallas kernels: 37.6 us -> 32.2 us  [optimizer(): pl.pallas_call(body, in_specs=[vmem] * 4 + [hbm] * (INS + count), out_spe...]
where the time goes in v3:
time: 404 us; the launch traced here: 398 us
  Pallas kernels  397 us (98%)
    pallas_call x1, Pallas kernels, reduce_and_start(): pl.pallas_call(functools.partial(reduce_body, depth, slots, early, parts,...  145 us
    pallas_call x1, Pallas kernels, gather(): pl.pallas_call(functools.partial(gather_body, depth, parts, [key for _, k...  127 us
    pallas_call x2, Pallas kernels, tower(): pl.pallas_call(functools.partial(tower_body, is_text, rows, slots), in_sp...  92.6 us
    pallas_call x1, Pallas kernels, optimizer(): pl.pallas_call(body, in_specs=[vmem] * 4 + [hbm] * (INS + count), out_spe...  32.2 us

profile of v3, /device:TPU:18, one launch (start us, length us, event | category | flops | bytes accessed | tf_op | source)
XLA Modules:
  0.0 397.9 jit_solution(5000538712412251900)
XLA Ops:
  0.6 127.0 %gather.1.copies = bf16[32,2064,256]{2,1,0:T(8,128)(2,1)} custom-call(f32[8,256,256]{2,1,0:T(8,128)} %refs_4_.3, f32[1,768]{1,0:T(1,128)} %refs_1_.3), custom_call_target="tpu_custom_call" | custom-call | tf_op jit(solution)/shard_map/gather/pallas_call | solution.py:927
  127.7 34.2 %image_tower.1 = (bf16[1,197,768]{2,1,0:T(8,128)(2,1)}, bf16[1,197,768]{2,1,0:T(8,128)(2,1)}, bf16[32,2064,256]{2,1,0:T(8,128)(2,1)}) custom-call(s32[234]{0:T(256)} %slot_ref.3, s32[32]{0:T(128)} %length_ref.3, bf16[1,197,768]{2,1,0:T(8,128)(2,1)} %x_ref.2, bf16[1,711,768]{2,1,0:T(8,128)(2,1)} %cot_ref.3, bf16[32,2064,256]{2,1,0:T(8,128)(2,1)} %gather.1.copies), custom_call_target="tpu_custom_call" | custom-call | tf_op jit(solution)/shard_map/image_tower/pallas_call | solution.py:444
  161.8 58.4 %text_tower.1 = (bf16[1,711,768]{2,1,0:T(8,128)(2,1)}, bf16[1,512,768]{2,1,0:T(8,128)(2,1)}, bf16[32,2064,256]{2,1,0:T(8,128)(2,1)}) custom-call(s32[234]{0:T(256)} %slot_ref.3, s32[32]{0:T(128)} %length_ref.3, bf16[1,512,768]{2,1,0:T(8,128)(2,1)} %x_ref.3, bf16[1,711,768]{2,1,0:T(8,128)(2,1)} %cot_ref.3, ...), custom_call_target="tpu_custom_call", output_to_operand_aliasing={{2}: (6, {})} | custom-call | tf_op jit(solution)/shard_map/text_tower/pallas_call | solution.py:444
  220.2 145.2 %reduce_and_start.1 = (f32[784,256]{1,0:T(8,128)}, f32[5,256,256]{2,1,0:T(8,128)}, f32[5,256,256]{2,1,0:T(8,128)}, f32[5,256,256]{2,1,0:T(8,128)}, f32[5,256,256...) custom-call(bf16[32,2064,256]{2,1,0:T(8,128)(2,1)} %get-tuple-element.42.grads_ref, ...), custom_call_target="tpu_custom_call" | custom-call | tf_op jit(solution)/shard_map/reduce_and_start/pallas_call | solution.py:1156
  365.4 32.2 %optimizer.1 = (f32[8,256,256]{2,1,0:T(8,128)}, f32[8,256,256]{2,1,0:T(8,128)}, f32[8,256,256]{2,1,0:T(8,128)}, f32[8,256,256]{2,1,0:T(8,128)}, f32[8,256,256]{2...) custom-call(f32[784,256]{1,0:T(8,128)} %get-tuple-element.43.refs_0_, ...), custom_call_target="tpu_custom_call" | custom-call | tf_op jit(solution)/shard_map/optimizer/pallas_call | solution.py:680

commit v4 on v3

--- a/solution.py
+++ b/solution.py
@@ -984,7 +984,7 @@
     for wave in range(2):
         for when, (part, *key) in timed + [(0.0, (part, 0, 0, 0)) for part in range(4)]:
             spent = end - when
-            at = spent * share if wave == 0 else end * (share - 0.06) + spent * (1 - share)
+            at = spent * share if wave == 0 else end * (share - 0.03) + spent * (1 - share)
             result.append((at, wave, -len(result), 4 * wave + part, tuple(key)))
     return [(part, key) for _, _, _, part, key in sorted(result)]
 

time: 404 us -> 407 us (level)
  no operation moved by 1% of the time
where the time goes in v4:
time: 407 us; the launch traced here: 401 us
  Pallas kernels  400 us (98%)
    pallas_call x1, Pallas kernels, reduce_and_start(): pl.pallas_call(functools.partial(reduce_body, depth, slots, early, parts,...  148 us
    pallas_call x1, Pallas kernels, gather(): pl.pallas_call(functools.partial(gather_body, depth, parts, [key for _, k...  127 us
    pallas_call x2, Pallas kernels, tower(): pl.pallas_call(functools.partial(tower_body, is_text, rows, slots), in_sp...  92.6 us
    pallas_call x1, Pallas kernels, optimizer(): pl.pallas_call(body, in_specs=[vmem] * 4 + [hbm] * (INS + count), out_spe...  32.2 us

profile of v4, /device:TPU:18, one launch (start us, length us, event | category | flops | bytes accessed | tf_op | source)
XLA Modules:
  0.0 400.6 jit_solution(7590838534011312566)
XLA Ops:
  0.6 127.0 %gather.1.copies = bf16[32,2064,256]{2,1,0:T(8,128)(2,1)} custom-call(f32[8,256,256]{2,1,0:T(8,128)} %refs_4_.3, f32[1,768]{1,0:T(1,128)} %refs_1_.3), custom_call_target="tpu_custom_call" | custom-call | tf_op jit(solution)/shard_map/gather/pallas_call | solution.py:927
  127.7 34.3 %image_tower.1 = (bf16[1,197,768]{2,1,0:T(8,128)(2,1)}, bf16[1,197,768]{2,1,0:T(8,128)(2,1)}, bf16[32,2064,256]{2,1,0:T(8,128)(2,1)}) custom-call(s32[234]{0:T(256)} %slot_ref.3, s32[32]{0:T(128)} %length_ref.3, bf16[1,197,768]{2,1,0:T(8,128)(2,1)} %x_ref.2, bf16[1,711,768]{2,1,0:T(8,128)(2,1)} %cot_ref.3, bf16[32,2064,256]{2,1,0:T(8,128)(2,1)} %gather.1.copies), custom_call_target="tpu_custom_call" | custom-call | tf_op jit(solution)/shard_map/image_tower/pallas_call | solution.py:444
  161.9 58.3 %text_tower.1 = (bf16[1,711,768]{2,1,0:T(8,128)(2,1)}, bf16[1,512,768]{2,1,0:T(8,128)(2,1)}, bf16[32,2064,256]{2,1,0:T(8,128)(2,1)}) custom-call(s32[234]{0:T(256)} %slot_ref.3, s32[32]{0:T(128)} %length_ref.3, bf16[1,512,768]{2,1,0:T(8,128)(2,1)} %x_ref.3, bf16[1,711,768]{2,1,0:T(8,128)(2,1)} %cot_ref.3, ...), custom_call_target="tpu_custom_call", output_to_operand_aliasing={{2}: (6, {})} | custom-call | tf_op jit(solution)/shard_map/text_tower/pallas_call | solution.py:444
  220.3 147.9 %reduce_and_start.1 = (f32[784,256]{1,0:T(8,128)}, f32[5,256,256]{2,1,0:T(8,128)}, f32[5,256,256]{2,1,0:T(8,128)}, f32[5,256,256]{2,1,0:T(8,128)}, f32[5,256,256...) custom-call(bf16[32,2064,256]{2,1,0:T(8,128)(2,1)} %get-tuple-element.42.grads_ref, ...), custom_call_target="tpu_custom_call" | custom-call | tf_op jit(solution)/shard_map/reduce_and_start/pallas_call | solution.py:1156
  368.2 32.2 %optimizer.1 = (f32[8,256,256]{2,1,0:T(8,128)}, f32[8,256,256]{2,1,0:T(8,128)}, f32[8,256,256]{2,1,0:T(8,128)}, f32[8,256,256]{2,1,0:T(8,128)}, f32[8,256,256]{2...) custom-call(f32[784,256]{1,0:T(8,128)} %get-tuple-element.43.refs_0_, ...), custom_call_target="tpu_custom_call" | custom-call | tf_op jit(solution)/shard_map/optimizer/pallas_call | solution.py:680
